TPU v7x, 32 devices: a whole 2x2x4 slice. The times are simulated.
32 devices in a mesh: dp: 8 (over y, x, core), tensor: 4 (over z).
Axes of the slice: x: 2, y: 2, z: 4, core: 2. Of those that a mesh axis runs over, the one named last changes fastest.
Arguments:
- hidden: bfloat16 [8, 1024, 4096], P('dp', None, 'tensor'), as said below
- gain: float32 [4096], replicated, may hold values from 0.5 to 1.5
- head: bfloat16 [4096, 16384], P(None, ('dp', 'tensor'))
- lengths: int32 [8], P('dp'), may hold values from 256 to 1024, as said below
- offsets: int32 [8, 32], P('dp'), may hold values from 0 to 255
- targets: int32 [8, 32], P('dp'), may hold values from 0 to 16383
- mask: int32 [8, 32], P('dp'), may hold values from 0 to 1, as said below
Outputs:
- logprob: float32 [8, 32], P('dp')
- entropy: float32 [8, 32], P('dp')
Inputs may be any that keep to these rules, and one draw needn't show every extreme that they name: `lengths`: each length is at least 256; some sequence has length exactly 1024 in every draw. `mask`: among the 32 slots of the sequences of one index of dp, at most 16 are scored; some index of dp has exactly 16. `hidden`: entries are of order one or a few tens in magnitude.
All inputs are finite; a program needn't handle non-finite values.
Results may differ from a plain program's by a relative error of at most 0.0089.
Values may be sent and summed in bfloat16 or wider, within the bound.
No kernel may reach another device: no remote copies, remote signals or barrier semaphores. Data moves between devices by JAX's collectives and lax.ppermute only.
A program may use at most 64 MiB of HBM per device.

v0:
```python
import functools

import jax
import jax.numpy as jnp
from jax import lax
from jax.experimental import pallas as pl
from jax.experimental.pallas import tpu as pltpu
from jax.sharding import PartitionSpec as P

LIVE = 16
SPAN = 256
BLOCK = 16
CODE = 128
DIGIT = 64
GROUP = 16


def vmem_limit(mebibytes):
    return pltpu.CompilerParams(vmem_limit_bytes=mebibytes * 1024 * 1024)


def in_hbm(x):
    return pltpu.with_memory_space_constraint(x, pltpu.HBM)


def pick_kernel(
    lengths, offsets, targets, mask, gain, hidden, rows, codes, place, gain_out, window, offset, target, alive, sems
):
    slot_count = offsets.shape[1]
    depth = window.shape[0]
    first = jnp.minimum((lengths[0] - SPAN) // BLOCK * BLOCK, hidden.shape[1] - depth)
    first = pl.multiple_of(first, BLOCK)
    copies = [
        pltpu.make_async_copy(offsets, offset, sems.at[0]),
        pltpu.make_async_copy(mask, alive, sems.at[1]),
        pltpu.make_async_copy(targets, target, sems.at[2]),
        pltpu.make_async_copy(gain, gain_out, sems.at[3]),
        pltpu.make_async_copy(hidden.at[0, pl.ds(first, depth)], window, sems.at[4]),
    ]
    for copy in copies:
        copy.start()
    for copy in copies[:2]:
        copy.wait()

    def iota(shape, axis):
        return lax.broadcasted_iota(jnp.int32, shape, axis)

    square = (slot_count, slot_count)
    live = jnp.where(alive[...] != 0, 1.0, 0.0)
    column = jnp.sum(jnp.where(iota(square, 0) == iota(square, 1), live, 0.0), axis=1, keepdims=True)
    rank = jnp.sum(jnp.where(iota(square, 0) < iota(square, 1), column, 0.0), axis=0, keepdims=True)
    wide = (LIVE, slot_count)
    chosen = jnp.where(iota(wide, 0).astype(jnp.float32) == rank, jnp.broadcast_to(live, wide), 0.0)
    place[...] = chosen
    offset_in = (lengths[0] - 1 - first) - offset[...]
    wanted = jnp.sum(chosen * (offset_in + 1).astype(jnp.float32), axis=1, keepdims=True) - 1.0
    select = jnp.where(iota((LIVE, depth), 1).astype(jnp.float32) == wanted, 1.0, 0.0).astype(jnp.bfloat16)
    copies[2].wait()
    ids = jnp.sum(chosen * target[...].astype(jnp.float32), axis=1, keepdims=True).astype(jnp.int32)
    lane = iota((LIVE, CODE), 1)
    digits = jnp.where(
        lane == 0, ids % DIGIT, jnp.where(lane == 1, (ids // DIGIT) % DIGIT, jnp.where(lane == 2, ids // (DIGIT * DIGIT), 0))
    )
    codes[...] = digits.astype(jnp.float32).astype(jnp.bfloat16)
    for copy in copies[3:]:
        copy.wait()
    rows[...] = jnp.dot(select, window[...], preferred_element_type=jnp.float32).astype(jnp.bfloat16)


def pick(hidden, gain, lengths, offsets, targets, mask):
    features = hidden.shape[2]
    slot_count = offsets.shape[1]
    vmem = pl.BlockSpec(memory_space=pltpu.VMEM)
    return pl.pallas_call(
        pick_kernel,
        out_shape=(
            jax.ShapeDtypeStruct((LIVE, features), jnp.bfloat16),
            jax.ShapeDtypeStruct((LIVE, CODE), jnp.bfloat16),
            jax.ShapeDtypeStruct((LIVE, slot_count), jnp.float32),
            jax.ShapeDtypeStruct((1, gain.shape[0]), jnp.float32),
        ),
        in_specs=[pl.BlockSpec(memory_space=pltpu.SMEM)] + [pl.BlockSpec(memory_space=pltpu.HBM)] * 5,
        out_specs=(vmem, vmem, vmem, vmem),
        scratch_shapes=[
            pltpu.VMEM((SPAN + BLOCK, features), jnp.bfloat16),
            pltpu.VMEM(offsets.shape, jnp.int32),
            pltpu.VMEM(offsets.shape, jnp.int32),
            pltpu.VMEM(offsets.shape, jnp.int32),
            pltpu.SemaphoreType.DMA((5,)),
        ],
        compiler_params=vmem_limit(32),
        name="pick",
    )(lengths, *map(in_hbm, (offsets, targets, mask, gain.reshape(1, -1), hidden)))


def join_kernel(*refs):
    tensor = len(refs) - 3
    parts, (codes, gain, rows) = refs[:tensor], refs[tensor:]
    live, features = parts[0].shape
    square = jnp.zeros((live, 1), jnp.float32)
    for part in parts:
        values = part[...].astype(jnp.float32)
        square += jnp.sum(values * values, axis=-1, keepdims=True)
    scale = lax.rsqrt(square / (tensor * features) + 1e-06)
    shard = lax.axis_index("tensor")
    for s, part in enumerate(parts):
        span = pl.ds(pl.multiple_of((shard ^ s) * features, features), features)
        rows[:, span] = (part[...].astype(jnp.float32) * scale * gain[:, span]).astype(jnp.bfloat16)
    rows[:, tensor * features :] = codes[...]


def join(parts, codes, gain):
    tensor = len(parts)
    live, features = parts[0].shape
    vmem = pl.BlockSpec(memory_space=pltpu.VMEM)
    return pl.pallas_call(
        join_kernel,
        out_shape=jax.ShapeDtypeStruct((live, tensor * features + CODE), jnp.bfloat16),
        in_specs=[vmem] * (tensor + 2),
        out_specs=vmem,
        compiler_params=vmem_limit(32),
        name="join",
    )(*parts, codes, gain)


def fetch_kernel(head, rows, held, rows_out, sems):
    count = sems.shape[0]
    depth = head.shape[0] // count
    copies = [
        pltpu.make_async_copy(head.at[pl.ds(i * depth, depth)], held.at[pl.ds(i * depth, depth)], sems.at[i])
        for i in range(count)
    ]
    for copy in copies:
        copy.start()
    rows_out[...] = rows[...]
    for copy in copies:
        copy.wait()


def fetch(head, rows):
    vmem = pl.BlockSpec(memory_space=pltpu.VMEM)
    return pl.pallas_call(
        fetch_kernel,
        out_shape=(pltpu.VMEM(head.shape, head.dtype), jax.ShapeDtypeStruct(rows.shape, rows.dtype)),
        in_specs=[pl.BlockSpec(memory_space=pltpu.HBM), vmem],
        out_specs=(vmem, vmem),
        scratch_shapes=[pltpu.SemaphoreType.DMA((4,))],
        compiler_params=vmem_limit(32),
        cost_estimate=pl.CostEstimate(flops=0, bytes_accessed=2 * head.size * 2, transcendentals=0),
        name="fetch",
    )(in_hbm(head), rows)


def score_kernel(*refs):
    dp = len(refs) - 2
    pieces, (head, stats) = refs[:dp], refs[dp:]
    depth, vocab_width = head.shape
    live = pieces[0].shape[0]
    row_count = dp * live
    mine = lax.axis_index("dp")
    start = (mine * stats.shape[1] + lax.axis_index("tensor")) * vocab_width

    normed = jnp.concatenate([piece[:, :depth] for piece in pieces], axis=0)
    logits = jnp.dot(normed, head[...], preferred_element_type=jnp.float32)
    digits = jnp.concatenate([piece[:, depth:] for piece in pieces], axis=0).astype(jnp.float32)
    lane = lax.broadcasted_iota(jnp.int32, (row_count, CODE), 1)
    weight = jnp.where(lane == 0, 1.0, jnp.where(lane == 1, float(DIGIT), jnp.where(lane == 2, float(DIGIT * DIGIT), 0.0)))
    target = jnp.sum(digits * weight, axis=-1, keepdims=True).astype(jnp.int32) - start
    column = lax.broadcasted_iota(jnp.int32, (row_count, vocab_width), 1)
    top = jnp.max(logits, axis=-1, keepdims=True)
    expo = jnp.exp(logits - top)
    total = jnp.sum(expo, axis=-1, keepdims=True)
    weighted = jnp.sum(expo * logits, axis=-1, keepdims=True)
    chosen = jnp.sum(jnp.where(column == target, logits, 0.0), axis=-1, keepdims=True)
    spot = lane - lax.broadcasted_iota(jnp.int32, (row_count, CODE), 0) % live
    table = jnp.zeros((row_count, CODE), jnp.float32)
    for group, value in enumerate((top, total, weighted, chosen)):
        table = jnp.where(spot == GROUP * group, value, table)
    for d in range(dp):
        line = jnp.sum(table[d * live : (d + 1) * live], axis=0, keepdims=True)
        for t in range(stats.shape[1]):
            stats[mine ^ d, t] = line


def score(pieces, head, copies):
    dp = len(pieces)
    live, width = pieces[0].shape
    vmem = pl.BlockSpec(memory_space=pltpu.VMEM)
    return pl.pallas_call(
        score_kernel,
        out_shape=jax.ShapeDtypeStruct((dp, copies, 1, CODE), jnp.float32),
        in_specs=[vmem] * (dp + 1),
        out_specs=vmem,
        compiler_params=vmem_limit(32),
        name="score",
    )(*pieces, pltpu.with_memory_space_constraint(head, pltpu.VMEM))


def combine(values):
    lane = lax.broadcasted_iota(jnp.int32, values.shape, 1)
    top = jnp.where(lane < GROUP, values, 0.0)
    top = top + pltpu.roll(top, GROUP, 1)
    top = top + pltpu.roll(top, 2 * GROUP, 1)
    best = jnp.max(top, axis=0, keepdims=True)
    factor = jnp.where(lane < 3 * GROUP, jnp.exp(top - best), 1.0)
    return jnp.sum(values * factor, axis=0, keepdims=True), best


def finish_kernel(stats, place, logprob, entropy, scored, spread, sems):
    sums, best = combine(stats[:, 0, :])
    total = pltpu.roll(sums, CODE - GROUP, 1)
    weighted = pltpu.roll(sums, CODE - 2 * GROUP, 1)
    chosen = pltpu.roll(sums, CODE - 3 * GROUP, 1)
    lse = best + jnp.log(total)
    lane = lax.broadcasted_iota(jnp.int32, (LIVE, CODE), 1)
    row = lax.broadcasted_iota(jnp.int32, (LIVE, CODE), 0)

    def to_slots(values):
        column = jnp.sum(jnp.where(lane == row, values, 0.0), axis=1, keepdims=True)
        return jnp.sum(place[...] * column, axis=0, keepdims=True)

    scored[...] = to_slots(chosen - lse)
    first = pltpu.make_async_copy(scored, logprob, sems.at[0])
    first.start()
    spread[...] = to_slots(lse - weighted / total)
    second = pltpu.make_async_copy(spread, entropy, sems.at[1])
    second.start()
    first.wait()
    second.wait()


def finish(stats, place, slot_count):
    vmem = pl.BlockSpec(memory_space=pltpu.VMEM)
    out = jax.ShapeDtypeStruct((1, slot_count), jnp.float32)
    return pl.pallas_call(
        finish_kernel,
        out_shape=(out, out),
        in_specs=[vmem, vmem],
        out_specs=[pl.BlockSpec(memory_space=pltpu.HBM)] * 2,
        scratch_shapes=[
            pltpu.VMEM((1, slot_count), jnp.float32),
            pltpu.VMEM((1, slot_count), jnp.float32),
            pltpu.SemaphoreType.DMA((2,)),
        ],
        compiler_params=vmem_limit(32),
        name="finish",
    )(stats, place)


def swap(x, axis, distance):
    return lax.ppermute(x, axis, [(i, i ^ distance) for i in range(lax.axis_size(axis))])


def per_device(hidden, gain, head, lengths, offsets, targets, mask):
    dp, tensor = lax.axis_size("dp"), lax.axis_size("tensor")
    rows, codes, slots, gain = pick(hidden, gain, lengths, offsets, targets, mask)
    parts = {0: rows} | {s: swap(rows, "tensor", s) for s in reversed(range(1, tensor))}
    rows = join([parts[s] for s in range(tensor)], codes, gain)

    pieces = {d: swap(rows, "dp", d) for d in reversed(range(2, dp, 2))}
    held, pieces[0] = fetch(head, rows)
    for d in range(0, dp, 2):
        pieces[d + 1] = swap(pieces[d], "dp", 1)
    stats = score([pieces[d] for d in range(dp)], held, tensor)
    stats = lax.all_to_all(stats.reshape(dp * tensor, 1, CODE), ("dp", "tensor"), 0, 0, tiled=True)
    return finish(stats, slots, offsets.shape[1])


def solution(mesh):
    return jax.shard_map(
        per_device,
        mesh=mesh,
        in_specs=(
            P("dp", None, "tensor"),
            P(),
            P(None, ("dp", "tensor")),
            P("dp"),
            P("dp", None),
            P("dp", None),
            P("dp", None),
        ),
        out_specs=(P("dp", None), P("dp", None)),
        check_vma=False,
    )
```

profile of v0, /device:TPU:0, one launch (start us, length us, event | category | flops | bytes accessed | tf_op | source)
XLA Modules:
  0.0 34.4 jit_solution(9216392220346382532)
XLA Ops:
  1.3 1.4 %pick.1 = (bf16[16,1024]{1,0:T(8,128)(2,1)S(1)}, bf16[16,128]{1,0:T(8,128)(2,1)S(1)}, f32[16,32]{1,0:T(8,128)S(1)}, f32[1,4096]{1,0:T(1,128)S(1)}) custom-call(s32[1]{0:T(128)S(6)} %copy.9.lengths, s32[1,32]{1,0:T(1,128)} %offsets.1, s32[1,32]{1,0:T(1,128)} %targets.1, s32[1,32]{1,0:T(1,128)} %mask.1, f32[1,4096]{1,0:T(1,128)} %bitcast.3, ...), custom_call_target="tpu_custom_call" | custom-call | tf_op jit(solution)/shard_map/pick/pallas_call | solution.py:74
  2.7 5.1 %collective-permute-start.2 = (bf16[16,1024]{1,0:T(8,128)(2,1)S(1)}, bf16[16,1024]{1,0:T(8,128)(2,1)S(1)}, u32[]{:S(2)}, u32[]{:S(2)}) collective-permute-start(bf16[16,1024]{1,0:T(8,128)(2,1)S(1)} %get-tuple-element.8.refs_0_), channel_id=1, source_target_pairs={{0,3},{1,2},{2,1},{3,0},{4,7},{5,6},{6,5},{7,4},{8,11},{9,10},{10,... | collective-permute-start | bytes 98312 | tf_op jit(solution)/shard_map/ppermute | solution.py:251
  7.8 0.0 collective-permute-start.1
  7.8 0.6 %collective-permute-start = (bf16[16,1024]{1,0:T(8,128)(2,1)S(1)}, bf16[16,1024]{1,0:T(8,128)(2,1)S(1)}, u32[]{:S(2)}, u32[]{:S(2)}) collective-permute-start(bf16[16,1024]{1,0:T(8,128)(2,1)S(1)} %get-tuple-element.8.refs_0_), channel_id=1, source_target_pairs={{0,1},{1,0},{2,3},{3,2},{4,5},{5,4},{6,7},{7,6},{8,9},{9,8},{10,11... | collective-permute-start | bytes 98312 | tf_op jit(solution)/shard_map/ppermute | solution.py:251
  8.4 1.3 %collective-permute-done.2.refs_3_ = bf16[16,1024]{1,0:T(8,128)(2,1)S(1)} collective-permute-done((bf16[16,1024]{1,0:T(8,128)(2,1)S(1)}, bf16[16,1024]{1,0:T(8,128)(2,1)S(1)}, u32[]{:S(2)}, u32[]{:S(2)}) %collective-permute-start.2) | collective-permute-done | bytes 32800 | tf_op jit(solution)/shard_map/ppermute | solution.py:251
  9.7 2.9 %collective-permute-done.1.refs_2_ = bf16[16,1024]{1,0:T(8,128)(2,1)S(1)} collective-permute-done((bf16[16,1024]{1,0:T(8,128)(2,1)S(1)}, bf16[16,1024]{1,0:T(8,128)(2,1)S(1)}, u32[]{:S(2)}, u32[]{:S(2)}) %collective-permute-start.1) | collective-permute-done | bytes 32800 | tf_op jit(solution)/shard_map/ppermute | solution.py:251
  12.6 0.0 collective-permute-done.refs_1_
  12.6 0.1 join.1.rows
  12.7 2.5 %collective-permute-start.8 = (bf16[16,4224]{1,0:T(8,128)(2,1)S(1)}, bf16[16,4224]{1,0:T(8,128)(2,1)S(1)}, u32[]{:S(2)}, u32[]{:S(2)}) collective-permute-start(bf16[16,4224]{1,0:T(8,128)(2,1)S(1)} %join.1.rows), channel_id=1, source_target_pairs={{0,24},{4,28},{8,16},{12,20},{16,8},{20,12},{24,0},{28,4},{1,25},{... | collective-permute-start | bytes 405512 | tf_op jit(solution)/shard_map/ppermute | solution.py:251
  15.2 0.5 %collective-permute-start.6 = (bf16[16,4224]{1,0:T(8,128)(2,1)S(1)}, bf16[16,4224]{1,0:T(8,128)(2,1)S(1)}, u32[]{:S(2)}, u32[]{:S(2)}) collective-permute-start(bf16[16,4224]{1,0:T(8,128)(2,1)S(1)} %join.1.rows), channel_id=1, source_target_pairs={{0,16},{4,20},{8,24},{12,28},{16,0},{20,4},{24,8},{28,12},{1,17},{... | collective-permute-start | bytes 405512 | tf_op jit(solution)/shard_map/ppermute | solution.py:251
  15.7 0.5 %collective-permute-start.4 = (bf16[16,4224]{1,0:T(8,128)(2,1)S(1)}, bf16[16,4224]{1,0:T(8,128)(2,1)S(1)}, u32[]{:S(2)}, u32[]{:S(2)}) collective-permute-start(bf16[16,4224]{1,0:T(8,128)(2,1)S(1)} %join.1.rows), channel_id=1, source_target_pairs={{0,8},{4,12},{8,0},{12,4},{16,24},{20,28},{24,16},{28,20},{1,9},{5... | collective-permute-start | bytes 405512 | tf_op jit(solution)/shard_map/ppermute | solution.py:251
  16.3 2.2 %fetch.1 = (bf16[4096,512]{1,0:T(8,128)(2,1)S(1)}, bf16[16,4224]{1,0:T(8,128)(2,1)S(1)}) custom-call(bf16[4096,512]{1,0:T(8,128)(2,1)} %head.1, bf16[16,4224]{1,0:T(8,128)(2,1)S(1)} %join.1.rows), custom_call_target="tpu_custom_call" | custom-call | bytes 8388608 | tf_op jit(solution)/shard_map/fetch/pallas_call | solution.py:142
  18.5 0.1 collective-permute-start.3
  18.6 1.6 %collective-permute-done.8.refs_6_ = bf16[16,4224]{1,0:T(8,128)(2,1)S(1)} collective-permute-done((bf16[16,4224]{1,0:T(8,128)(2,1)S(1)}, bf16[16,4224]{1,0:T(8,128)(2,1)S(1)}, u32[]{:S(2)}, u32[]{:S(2)}) %collective-permute-start.8) | collective-permute-done | bytes 135200 | tf_op jit(solution)/shard_map/ppermute | solution.py:251
  20.1 0.0 collective-permute-start.9
  20.2 0.8 %collective-permute-done.6.refs_4_ = bf16[16,4224]{1,0:T(8,128)(2,1)S(1)} collective-permute-done((bf16[16,4224]{1,0:T(8,128)(2,1)S(1)}, bf16[16,4224]{1,0:T(8,128)(2,1)S(1)}, u32[]{:S(2)}, u32[]{:S(2)}) %collective-permute-start.6) | collective-permute-done | bytes 135200 | tf_op jit(solution)/shard_map/ppermute | solution.py:251
  20.9 0.0 collective-permute-start.7
  20.9 0.0 collective-permute-done.4.refs_2_
  20.9 0.5 %collective-permute-start.5 = (bf16[16,4224]{1,0:T(8,128)(2,1)S(1)}, bf16[16,4224]{1,0:T(8,128)(2,1)S(1)}, u32[]{:S(2)}, u32[]{:S(2)}) collective-permute-start(bf16[16,4224]{1,0:T(8,128)(2,1)S(1)} %collective-permute-done.4.refs_2_), channel_id=1, source_target_pairs={{0,4},{4,0},{8,12},{12,8},{16,20},{20,16},{24,28},{28,24},{1,5},{5... | collective-permute-start | bytes 405512 | tf_op jit(solution)/shard_map/ppermute | solution.py:251
  21.4 0.0 collective-permute-done.3.refs_1_
  21.4 0.1 collective-permute-done.9.refs_7_
  21.5 0.8 %collective-permute-done.7.refs_5_ = bf16[16,4224]{1,0:T(8,128)(2,1)S(1)} collective-permute-done((bf16[16,4224]{1,0:T(8,128)(2,1)S(1)}, bf16[16,4224]{1,0:T(8,128)(2,1)S(1)}, u32[]{:S(2)}, u32[]{:S(2)}) %collective-permute-start.7) | collective-permute-done | bytes 135200 | tf_op jit(solution)/shard_map/ppermute | solution.py:251
  22.3 0.2 collective-permute-done.5.refs_3_
  22.5 0.9 %score.1 = f32[8,4,1,128]{3,2,1,0:T(1,128)S(1)} custom-call(bf16[16,4224]{1,0:T(8,128)(2,1)S(1)} %get-tuple-element.11.refs_0_, bf16[16,4224]{1,0:T(8,128)(2,1)S(1)} %collective-permute-done.3.refs_1_, bf16[16,4224]{1,0:T(8,128)(2,1)S(1)} %collective-permute-done.4.refs_2_, bf16[16,4224]{1,0:T(8,128)(2,1)S(1)} %collective-permute-done.5.refs_3_, ...), custom_call_target="tpu_custom_call" | custom-call | tf_op jit(solution)/shard_map/score/pallas_call | solution.py:189
  23.4 10.1 %all_to_all.5.stats = f32[32,1,128]{2,1,0:T(1,128)S(1)} all-to-all(f32[32,1,128]{2,1,0:T(1,128)S(1)} %bitcast.2), channel_id=1, replica_groups=mesh['dp'=8,'tensor'=4] {'dp','tensor'}, dimensions={0} | all-to-all | bytes 32768 | tf_op jit(solution)/shard_map/all_to_all | solution.py:265
  33.5 0.9 %finish.1 = (f32[1,32]{1,0:T(1,128)}, f32[1,32]{1,0:T(1,128)}) custom-call(f32[32,1,128]{2,1,0:T(1,128)S(1)} %all_to_all.5.stats, f32[16,32]{1,0:T(8,128)S(1)} %get-tuple-element.13.place), custom_call_target="tpu_custom_call" | custom-call | tf_op jit(solution)/shard_map/finish/pallas_call | solution.py:235
Async XLA Ops:
  2.7 7.0 %collective-permute-start.2 = (bf16[16,1024]{1,0:T(8,128)(2,1)S(1)}, bf16[16,1024]{1,0:T(8,128)(2,1)S(1)}, u32[]{:S(2)}, u32[]{:S(2)}) collective-permute-start(bf16[16,1024]{1,0:T(8,128)(2,1)S(1)} %get-tuple-element.8.refs_0_), channel_id=1, source_target_pairs={{0,3},{1,2},{2,1},{3,0},{4,7},{5,6},{6,5},{7,4},{8,11},{9,10},{10,... | collective-permute-start | bytes 98312 | tf_op jit(solution)/shard_map/ppermute | solution.py:251
  7.8 4.8 %collective-permute-start.1 = (bf16[16,1024]{1,0:T(8,128)(2,1)S(1)}, bf16[16,1024]{1,0:T(8,128)(2,1)S(1)}, u32[]{:S(2)}, u32[]{:S(2)}) collective-permute-start(bf16[16,1024]{1,0:T(8,128)(2,1)S(1)} %get-tuple-element.8.refs_0_), channel_id=1, source_target_pairs={{0,2},{1,3},{2,0},{3,1},{4,6},{5,7},{6,4},{7,5},{8,10},{9,11},{10,... | collective-permute-start | bytes 98312 | tf_op jit(solution)/shard_map/ppermute | solution.py:251
  7.8 4.8 %collective-permute-start = (bf16[16,1024]{1,0:T(8,128)(2,1)S(1)}, bf16[16,1024]{1,0:T(8,128)(2,1)S(1)}, u32[]{:S(2)}, u32[]{:S(2)}) collective-permute-start(bf16[16,1024]{1,0:T(8,128)(2,1)S(1)} %get-tuple-element.8.refs_0_), channel_id=1, source_target_pairs={{0,1},{1,0},{2,3},{3,2},{4,5},{5,4},{6,7},{7,6},{8,9},{9,8},{10,11... | collective-permute-start | bytes 98312 | tf_op jit(solution)/shard_map/ppermute | solution.py:251
  12.7 7.4 %collective-permute-start.8 = (bf16[16,4224]{1,0:T(8,128)(2,1)S(1)}, bf16[16,4224]{1,0:T(8,128)(2,1)S(1)}, u32[]{:S(2)}, u32[]{:S(2)}) collective-permute-start(bf16[16,4224]{1,0:T(8,128)(2,1)S(1)} %join.1.rows), channel_id=1, source_target_pairs={{0,24},{4,28},{8,16},{12,20},{16,8},{20,12},{24,0},{28,4},{1,25},{... | collective-permute-start | bytes 405512 | tf_op jit(solution)/shard_map/ppermute | solution.py:251
  15.2 5.7 %collective-permute-start.6 = (bf16[16,4224]{1,0:T(8,128)(2,1)S(1)}, bf16[16,4224]{1,0:T(8,128)(2,1)S(1)}, u32[]{:S(2)}, u32[]{:S(2)}) collective-permute-start(bf16[16,4224]{1,0:T(8,128)(2,1)S(1)} %join.1.rows), channel_id=1, source_target_pairs={{0,16},{4,20},{8,24},{12,28},{16,0},{20,4},{24,8},{28,12},{1,17},{... | collective-permute-start | bytes 405512 | tf_op jit(solution)/shard_map/ppermute | solution.py:251
  15.7 5.2 %collective-permute-start.4 = (bf16[16,4224]{1,0:T(8,128)(2,1)S(1)}, bf16[16,4224]{1,0:T(8,128)(2,1)S(1)}, u32[]{:S(2)}, u32[]{:S(2)}) collective-permute-start(bf16[16,4224]{1,0:T(8,128)(2,1)S(1)} %join.1.rows), channel_id=1, source_target_pairs={{0,8},{4,12},{8,0},{12,4},{16,24},{20,28},{24,16},{28,20},{1,9},{5... | collective-permute-start | bytes 405512 | tf_op jit(solution)/shard_map/ppermute | solution.py:251
  18.5 2.9 %collective-permute-start.3 = (bf16[16,4224]{1,0:T(8,128)(2,1)S(1)}, bf16[16,4224]{1,0:T(8,128)(2,1)S(1)}, u32[]{:S(2)}, u32[]{:S(2)}) collective-permute-start(bf16[16,4224]{1,0:T(8,128)(2,1)S(1)} %get-tuple-element.11.refs_0_), channel_id=1, source_target_pairs={{0,4},{4,0},{8,12},{12,8},{16,20},{20,16},{24,28},{28,24},{1,5},{5... | collective-permute-start | bytes 405512 | tf_op jit(solution)/shard_map/ppermute | solution.py:251
  20.1 1.4 %collective-permute-start.9 = (bf16[16,4224]{1,0:T(8,128)(2,1)S(1)}, bf16[16,4224]{1,0:T(8,128)(2,1)S(1)}, u32[]{:S(2)}, u32[]{:S(2)}) collective-permute-start(bf16[16,4224]{1,0:T(8,128)(2,1)S(1)} %collective-permute-done.8.refs_6_), channel_id=1, source_target_pairs={{0,4},{4,0},{8,12},{12,8},{16,20},{20,16},{24,28},{28,24},{1,5},{5... | collective-permute-start | bytes 405512 | tf_op jit(solution)/shard_map/ppermute | solution.py:251
  20.9 1.4 %collective-permute-start.7 = (bf16[16,4224]{1,0:T(8,128)(2,1)S(1)}, bf16[16,4224]{1,0:T(8,128)(2,1)S(1)}, u32[]{:S(2)}, u32[]{:S(2)}) collective-permute-start(bf16[16,4224]{1,0:T(8,128)(2,1)S(1)} %collective-permute-done.6.refs_4_), channel_id=1, source_target_pairs={{0,4},{4,0},{8,12},{12,8},{16,20},{20,16},{24,28},{28,24},{1,5},{5... | collective-permute-start | bytes 405512 | tf_op jit(solution)/shard_map/ppermute | solution.py:251
  20.9 1.5 %collective-permute-start.5 = (bf16[16,4224]{1,0:T(8,128)(2,1)S(1)}, bf16[16,4224]{1,0:T(8,128)(2,1)S(1)}, u32[]{:S(2)}, u32[]{:S(2)}) collective-permute-start(bf16[16,4224]{1,0:T(8,128)(2,1)S(1)} %collective-permute-done.4.refs_2_), channel_id=1, source_target_pairs={{0,4},{4,0},{8,12},{12,8},{16,20},{20,16},{24,28},{28,24},{1,5},{5... | collective-permute-start | bytes 405512 | tf_op jit(solution)/shard_map/ppermute | solution.py:251
where the time goes:
time: 34.6 us; the launch traced here: 34.4 us
  blocking collectives  10.1 us (29%)
  starting transfers between devices  9.89 us (29%)
  waiting for transfers between devices  7.55 us (22%)
  Pallas kernels  5.48 us (16%)
  between operations  1.32 us (4%)
    all_to_all x1, blocking collectives, per_device(): lax.all_to_all(stats.reshape(dp * tensor, 1, CODE), ('dp', 'tensor'), 0,...  10.1 us
    ppermute x10, starting transfers between devices, swap(): lax.ppermute(x, axis, [(i, i ^ distance) for i in range(lax.axis_size(axi...  9.89 us
    ppermute x10, waiting for transfers between devices, swap(): lax.ppermute(x, axis, [(i, i ^ distance) for i in range(lax.axis_size(axi...  7.55 us
    pallas_call x1, Pallas kernels, fetch(): pl.pallas_call(fetch_kernel, out_shape=(pltpu.VMEM(head.shape, head.dtype...  2.21 us
    pallas_call x1, Pallas kernels, pick(): pl.pallas_call(pick_kernel, out_shape=(jax.ShapeDtypeStruct((LIVE, featur...  1.37 us
    pallas_call x1, Pallas kernels, score(): pl.pallas_call(score_kernel, out_shape=jax.ShapeDtypeStruct((dp, copies,...  0.9 us
    pallas_call x1, Pallas kernels, finish(): pl.pallas_call(finish_kernel, out_shape=(out, out), in_specs=[vmem, vmem]...  0.87 us
  transfers between devices with their start and end apart: 10, of which 7 were waited for; matrix products, arithmetic and copies ran while one was open for 0% of the time, Pallas kernels for 6%

commit v1 on v0

--- a/solution.py
+++ b/solution.py
@@ -93,34 +93,41 @@
     )(lengths, *map(in_hbm, (offsets, targets, mask, gain.reshape(1, -1), hidden)))
 
 
-def join_kernel(*refs):
-    tensor = len(refs) - 3
-    parts, (codes, gain, rows) = refs[:tensor], refs[tensor:]
-    live, features = parts[0].shape
-    square = jnp.zeros((live, 1), jnp.float32)
-    for part in parts:
-        values = part[...].astype(jnp.float32)
-        square += jnp.sum(values * values, axis=-1, keepdims=True)
+def join_kernel(tensor, *refs):
+    pieces, (codes, gain, rows) = refs[:-3][::-1], refs[-3:]
+    own, turned, paired = pieces[0], pieces[1 : tensor - 1], pieces[tensor - 1 :]
+    live, features = own.shape
+    shard = lax.axis_index("tensor")
+    final = tensor - 1
+
+    parts = [(shard, own[...].astype(jnp.float32))]
+    for r, (around, pair) in enumerate(zip(turned, paired), 1):
+        source = jnp.where(shard == final, r - 1, lax.rem(shard + final - r, final))
+        parts.append((source, jnp.where(shard == final, pair[...], around[...]).astype(jnp.float32)))
+    left = paired[final - 1][...]
+    for i, pair in enumerate(paired[:-1]):
+        left = jnp.where(shard == i, pair[...], left)
+    parts.append((jnp.where(shard == final, final - 1, final), left.astype(jnp.float32)))
+
+    square = sum(jnp.sum(values * values, axis=-1, keepdims=True) for _, values in parts)
     scale = lax.rsqrt(square / (tensor * features) + 1e-06)
-    shard = lax.axis_index("tensor")
-    for s, part in enumerate(parts):
-        span = pl.ds(pl.multiple_of((shard ^ s) * features, features), features)
-        rows[:, span] = (part[...].astype(jnp.float32) * scale * gain[:, span]).astype(jnp.bfloat16)
+    for source, values in parts:
+        span = pl.ds(pl.multiple_of(source * features, features), features)
+        rows[:, span] = (values * scale * gain[:, span]).astype(jnp.bfloat16)
     rows[:, tensor * features :] = codes[...]
 
 
-def join(parts, codes, gain):
-    tensor = len(parts)
-    live, features = parts[0].shape
-    vmem = pl.BlockSpec(memory_space=pltpu.VMEM)
-    return pl.pallas_call(
-        join_kernel,
+def join(pieces, tensor, codes, gain):
+    live, features = pieces[0].shape
+    vmem = pl.BlockSpec(memory_space=pltpu.VMEM)
+    return pl.pallas_call(
+        functools.partial(join_kernel, tensor),
         out_shape=jax.ShapeDtypeStruct((live, tensor * features + CODE), jnp.bfloat16),
-        in_specs=[vmem] * (tensor + 2),
+        in_specs=[vmem] * (len(pieces) + 2),
         out_specs=vmem,
         compiler_params=vmem_limit(32),
         name="join",
-    )(*parts, codes, gain)
+    )(*reversed(pieces), codes, gain)
 
 
 def fetch_kernel(head, rows, held, rows_out, sems):
@@ -254,8 +261,10 @@
 def per_device(hidden, gain, head, lengths, offsets, targets, mask):
     dp, tensor = lax.axis_size("dp"), lax.axis_size("tensor")
     rows, codes, slots, gain = pick(hidden, gain, lengths, offsets, targets, mask)
-    parts = {0: rows} | {s: swap(rows, "tensor", s) for s in reversed(range(1, tensor))}
-    rows = join([parts[s] for s in range(tensor)], codes, gain)
+    final = tensor - 1
+    pairs = [[(i, (i + r) % final) for i in range(final)] + [(final, final)] for r in range(1, final)]
+    pairs += [[(i, final), (final, i)] + [(j, j) for j in range(final) if j != i] for i in range(final)]
+    rows = join([rows] + [lax.ppermute(rows, "tensor", pair) for pair in pairs], tensor, codes, gain)
 
     pieces = {d: swap(rows, "dp", d) for d in reversed(range(2, dp, 2))}
     held, pieces[0] = fetch(head, rows)

time: 34.6 us -> 44.2 us (1.28)
  starting transfers between devices: 9.89 us -> 15.2 us
  blocking collectives: 10.1 us -> 13.9 us
    ppermute x0 -> x5, starting transfers between devices: none -> 11.1 us  [per_device(): lax.ppermute(rows, 'tensor', pair)]
    ppermute x10 -> x7, starting transfers between devices: 9.89 us -> 4.13 us  [swap(): lax.ppermute(x, axis, [(i, i ^ distance) for i in range(lax.axis_size(axi...]
    ppermute x0 -> x5, waiting for transfers between devices: none -> 4.33 us  [per_device(): lax.ppermute(rows, 'tensor', pair)]
    ppermute x10 -> x7, waiting for transfers between devices: 7.55 us -> 3.6 us  [swap(): lax.ppermute(x, axis, [(i, i ^ distance) for i in range(lax.axis_size(axi...]
    all_to_all x1, blocking collectives: 10.1 us -> 13.9 us  [per_device(): lax.all_to_all(stats.reshape(dp * tensor, 1, CODE), ('dp', 'tensor'), 0,...]
  transfers between devices with their start and end apart: 10 -> 12, of which waited for: 7 -> 5; matrix products, arithmetic and copies ran while one was open for 0% -> 0% of each run, Pallas kernels for 6% -> 5%
where the time goes in v1:
time: 44.2 us; the launch traced here: 44 us
  starting transfers between devices  15.2 us (34%)
  blocking collectives  13.9 us (31%)
  waiting for transfers between devices  7.93 us (18%)
  Pallas kernels  5.49 us (12%)
  between operations  1.38 us (3%)
    all_to_all x1, blocking collectives, per_device(): lax.all_to_all(stats.reshape(dp * tensor, 1, CODE), ('dp', 'tensor'), 0,...  13.9 us
    ppermute x5, starting transfers between devices, per_device(): lax.ppermute(rows, 'tensor', pair)  11.1 us
    ppermute x5, waiting for transfers between devices, per_device(): lax.ppermute(rows, 'tensor', pair)  4.33 us
    ppermute x7, starting transfers between devices, swap(): lax.ppermute(x, axis, [(i, i ^ distance) for i in range(lax.axis_size(axi...  4.13 us
    ppermute x7, waiting for transfers between devices, swap(): lax.ppermute(x, axis, [(i, i ^ distance) for i in range(lax.axis_size(axi...  3.6 us
    pallas_call x1, Pallas kernels, fetch(): pl.pallas_call(fetch_kernel, out_shape=(pltpu.VMEM(head.shape, head.dtype...  2.21 us
    pallas_call x1, Pallas kernels, pick(): pl.pallas_call(pick_kernel, out_shape=(jax.ShapeDtypeStruct((LIVE, featur...  1.37 us
    pallas_call x1, Pallas kernels, score(): pl.pallas_call(score_kernel, out_shape=jax.ShapeDtypeStruct((dp, copies,...  0.9 us
  transfers between devices with their start and end apart: 12, of which 5 were waited for; matrix products, arithmetic and copies ran while one was open for 0% of the time, Pallas kernels for 5%

profile of v1, /device:TPU:0, one launch (start us, length us, event | category | flops | bytes accessed | tf_op | source)
XLA Modules:
  0.0 44.0 jit_solution(63465588663323359)
XLA Ops:
  1.3 1.4 %pick.1 = (bf16[16,1024]{1,0:T(8,128)(2,1)S(1)}, bf16[16,128]{1,0:T(8,128)(2,1)S(1)}, f32[16,32]{1,0:T(8,128)S(1)}, f32[1,4096]{1,0:T(1,128)S(1)}) custom-call(s32[1]{0:T(128)S(6)} %copy.9.lengths, s32[1,32]{1,0:T(1,128)} %offsets.1, s32[1,32]{1,0:T(1,128)} %targets.1, s32[1,32]{1,0:T(1,128)} %mask.1, f32[1,4096]{1,0:T(1,128)} %bitcast.3, ...), custom_call_target="tpu_custom_call" | custom-call | tf_op jit(solution)/shard_map/pick/pallas_call | solution.py:74
  2.7 4.9 %collective-permute-start.4 = (bf16[16,1024]{1,0:T(8,128)(2,1)S(1)}, bf16[16,1024]{1,0:T(8,128)(2,1)S(1)}, u32[]{:S(2)}, u32[]{:S(2)}) collective-permute-start(bf16[16,1024]{1,0:T(8,128)(2,1)S(1)} %get-tuple-element.8.refs_5_), channel_id=1, source_target_pairs={{0,1},{1,2},{2,0},{3,3},{4,5},{5,6},{6,4},{7,7},{8,9},{9,10},{10,8... | collective-permute-start | bytes 98312 | tf_op jit(solution)/shard_map/ppermute | solution.py:267
  7.6 2.9 %collective-permute-start.3 = (bf16[16,1024]{1,0:T(8,128)(2,1)S(1)}, bf16[16,1024]{1,0:T(8,128)(2,1)S(1)}, u32[]{:S(2)}, u32[]{:S(2)}) collective-permute-start(bf16[16,1024]{1,0:T(8,128)(2,1)S(1)} %get-tuple-element.8.refs_5_), channel_id=1, source_target_pairs={{0,2},{1,0},{2,1},{3,3},{4,6},{5,4},{6,5},{7,7},{8,10},{9,8},{10,9... | collective-permute-start | bytes 98312 | tf_op jit(solution)/shard_map/ppermute | solution.py:267
  10.5 1.9 %collective-permute-start.2 = (bf16[16,1024]{1,0:T(8,128)(2,1)S(1)}, bf16[16,1024]{1,0:T(8,128)(2,1)S(1)}, u32[]{:S(2)}, u32[]{:S(2)}) collective-permute-start(bf16[16,1024]{1,0:T(8,128)(2,1)S(1)} %get-tuple-element.8.refs_5_), channel_id=1, source_target_pairs={{0,3},{3,0},{1,1},{2,2},{4,7},{7,4},{5,5},{6,6},{8,11},{11,8},{9,9... | collective-permute-start | bytes 98312 | tf_op jit(solution)/shard_map/ppermute | solution.py:267
  12.5 0.7 %collective-permute-start.1 = (bf16[16,1024]{1,0:T(8,128)(2,1)S(1)}, bf16[16,1024]{1,0:T(8,128)(2,1)S(1)}, u32[]{:S(2)}, u32[]{:S(2)}) collective-permute-start(bf16[16,1024]{1,0:T(8,128)(2,1)S(1)} %get-tuple-element.8.refs_5_), channel_id=1, source_target_pairs={{1,3},{3,1},{0,0},{2,2},{5,7},{7,5},{4,4},{6,6},{9,11},{11,9},{8,8... | collective-permute-start | bytes 98312 | tf_op jit(solution)/shard_map/ppermute | solution.py:267
  13.1 0.7 %collective-permute-start = (bf16[16,1024]{1,0:T(8,128)(2,1)S(1)}, bf16[16,1024]{1,0:T(8,128)(2,1)S(1)}, u32[]{:S(2)}, u32[]{:S(2)}) collective-permute-start(bf16[16,1024]{1,0:T(8,128)(2,1)S(1)} %get-tuple-element.8.refs_5_), channel_id=1, source_target_pairs={{2,3},{3,2},{0,0},{1,1},{6,7},{7,6},{4,4},{5,5},{10,11},{11,10},{8... | collective-permute-start | bytes 98312 | tf_op jit(solution)/shard_map/ppermute | solution.py:267
  13.8 0.0 collective-permute-done.4.refs_4_
  13.8 0.0 collective-permute-done.3.refs_3_
  13.8 4.3 %collective-permute-done.2.refs_2_ = bf16[16,1024]{1,0:T(8,128)(2,1)S(1)} collective-permute-done((bf16[16,1024]{1,0:T(8,128)(2,1)S(1)}, bf16[16,1024]{1,0:T(8,128)(2,1)S(1)}, u32[]{:S(2)}, u32[]{:S(2)}) %collective-permute-start.2) | collective-permute-done | bytes 32800 | tf_op jit(solution)/shard_map/ppermute | solution.py:267
  18.1 0.0 collective-permute-done.1.refs_1_
  18.1 0.0 collective-permute-done.refs_0_
  18.1 0.1 join.1.rows
  18.3 3.0 %collective-permute-start.10 = (bf16[16,4224]{1,0:T(8,128)(2,1)S(1)}, bf16[16,4224]{1,0:T(8,128)(2,1)S(1)}, u32[]{:S(2)}, u32[]{:S(2)}) collective-permute-start(bf16[16,4224]{1,0:T(8,128)(2,1)S(1)} %join.1.rows), channel_id=1, source_target_pairs={{0,24},{4,28},{8,16},{12,20},{16,8},{20,12},{24,0},{28,4},{1,25},{... | collective-permute-start | bytes 405512 | tf_op jit(solution)/shard_map/ppermute | solution.py:258
  21.3 0.5 %collective-permute-start.8 = (bf16[16,4224]{1,0:T(8,128)(2,1)S(1)}, bf16[16,4224]{1,0:T(8,128)(2,1)S(1)}, u32[]{:S(2)}, u32[]{:S(2)}) collective-permute-start(bf16[16,4224]{1,0:T(8,128)(2,1)S(1)} %join.1.rows), channel_id=1, source_target_pairs={{0,16},{4,20},{8,24},{12,28},{16,0},{20,4},{24,8},{28,12},{1,17},{... | collective-permute-start | bytes 405512 | tf_op jit(solution)/shard_map/ppermute | solution.py:258
  21.8 0.1 collective-permute-start.6
  21.9 2.2 %fetch.1 = (bf16[4096,512]{1,0:T(8,128)(2,1)S(1)}, bf16[16,4224]{1,0:T(8,128)(2,1)S(1)}) custom-call(bf16[4096,512]{1,0:T(8,128)(2,1)} %head.1, bf16[16,4224]{1,0:T(8,128)(2,1)S(1)} %join.1.rows), custom_call_target="tpu_custom_call" | custom-call | bytes 8388608 | tf_op jit(solution)/shard_map/fetch/pallas_call | solution.py:149
  24.1 0.1 collective-permute-start.5
  24.2 1.6 %collective-permute-done.10.refs_6_ = bf16[16,4224]{1,0:T(8,128)(2,1)S(1)} collective-permute-done((bf16[16,4224]{1,0:T(8,128)(2,1)S(1)}, bf16[16,4224]{1,0:T(8,128)(2,1)S(1)}, u32[]{:S(2)}, u32[]{:S(2)}) %collective-permute-start.10) | collective-permute-done | bytes 135200 | tf_op jit(solution)/shard_map/ppermute | solution.py:258
  25.8 0.0 collective-permute-start.11
  25.8 1.0 %collective-permute-done.8.refs_4_ = bf16[16,4224]{1,0:T(8,128)(2,1)S(1)} collective-permute-done((bf16[16,4224]{1,0:T(8,128)(2,1)S(1)}, bf16[16,4224]{1,0:T(8,128)(2,1)S(1)}, u32[]{:S(2)}, u32[]{:S(2)}) %collective-permute-start.8) | collective-permute-done | bytes 135200 | tf_op jit(solution)/shard_map/ppermute | solution.py:258
  26.7 0.0 collective-permute-start.9
  26.7 0.0 collective-permute-done.6.refs_2_
  26.8 0.5 %collective-permute-start.7 = (bf16[16,4224]{1,0:T(8,128)(2,1)S(1)}, bf16[16,4224]{1,0:T(8,128)(2,1)S(1)}, u32[]{:S(2)}, u32[]{:S(2)}) collective-permute-start(bf16[16,4224]{1,0:T(8,128)(2,1)S(1)} %collective-permute-done.6.refs_2_), channel_id=1, source_target_pairs={{0,4},{4,0},{8,12},{12,8},{16,20},{20,16},{24,28},{28,24},{1,5},{5... | collective-permute-start | bytes 405512 | tf_op jit(solution)/shard_map/ppermute | solution.py:258
  27.2 0.0 collective-permute-done.5.refs_1_
  27.2 0.0 collective-permute-done.11.refs_7_
  27.2 0.8 %collective-permute-done.9.refs_5_ = bf16[16,4224]{1,0:T(8,128)(2,1)S(1)} collective-permute-done((bf16[16,4224]{1,0:T(8,128)(2,1)S(1)}, bf16[16,4224]{1,0:T(8,128)(2,1)S(1)}, u32[]{:S(2)}, u32[]{:S(2)}) %collective-permute-start.9) | collective-permute-done | bytes 135200 | tf_op jit(solution)/shard_map/ppermute | solution.py:258
  28.1 0.2 collective-permute-done.7.refs_3_
  28.3 0.9 %score.1 = f32[8,4,1,128]{3,2,1,0:T(1,128)S(1)} custom-call(bf16[16,4224]{1,0:T(8,128)(2,1)S(1)} %get-tuple-element.11.refs_0_, bf16[16,4224]{1,0:T(8,128)(2,1)S(1)} %collective-permute-done.5.refs_1_, bf16[16,4224]{1,0:T(8,128)(2,1)S(1)} %collective-permute-done.6.refs_2_, bf16[16,4224]{1,0:T(8,128)(2,1)S(1)} %collective-permute-done.7.refs_3_, ...), custom_call_target="tpu_custom_call" | custom-call | tf_op jit(solution)/shard_map/score/pallas_call | solution.py:196
  29.2 13.9 %all_to_all.5.stats = f32[32,1,128]{2,1,0:T(1,128)S(1)} all-to-all(f32[32,1,128]{2,1,0:T(1,128)S(1)} %bitcast.2), channel_id=1, replica_groups=mesh['dp'=8,'tensor'=4] {'dp','tensor'}, dimensions={0} | all-to-all | bytes 32768 | tf_op jit(solution)/shard_map/all_to_all | solution.py:274
  43.1 0.9 %finish.1 = (f32[1,32]{1,0:T(1,128)}, f32[1,32]{1,0:T(1,128)}) custom-call(f32[32,1,128]{2,1,0:T(1,128)S(1)} %all_to_all.5.stats, f32[16,32]{1,0:T(8,128)S(1)} %get-tuple-element.13.place), custom_call_target="tpu_custom_call" | custom-call | tf_op jit(solution)/shard_map/finish/pallas_call | solution.py:242
Async XLA Ops:
  2.7 11.2 %collective-permute-start.4 = (bf16[16,1024]{1,0:T(8,128)(2,1)S(1)}, bf16[16,1024]{1,0:T(8,128)(2,1)S(1)}, u32[]{:S(2)}, u32[]{:S(2)}) collective-permute-start(bf16[16,1024]{1,0:T(8,128)(2,1)S(1)} %get-tuple-element.8.refs_5_), channel_id=1, source_target_pairs={{0,1},{1,2},{2,0},{3,3},{4,5},{5,6},{6,4},{7,7},{8,9},{9,10},{10,8... | collective-permute-start | bytes 98312 | tf_op jit(solution)/shard_map/ppermute | solution.py:267
  7.6 6.2 %collective-permute-start.3 = (bf16[16,1024]{1,0:T(8,128)(2,1)S(1)}, bf16[16,1024]{1,0:T(8,128)(2,1)S(1)}, u32[]{:S(2)}, u32[]{:S(2)}) collective-permute-start(bf16[16,1024]{1,0:T(8,128)(2,1)S(1)} %get-tuple-element.8.refs_5_), channel_id=1, source_target_pairs={{0,2},{1,0},{2,1},{3,3},{4,6},{5,4},{6,5},{7,7},{8,10},{9,8},{10,9... | collective-permute-start | bytes 98312 | tf_op jit(solution)/shard_map/ppermute | solution.py:267
  10.5 7.6 %collective-permute-start.2 = (bf16[16,1024]{1,0:T(8,128)(2,1)S(1)}, bf16[16,1024]{1,0:T(8,128)(2,1)S(1)}, u32[]{:S(2)}, u32[]{:S(2)}) collective-permute-start(bf16[16,1024]{1,0:T(8,128)(2,1)S(1)} %get-tuple-element.8.refs_5_), channel_id=1, source_target_pairs={{0,3},{3,0},{1,1},{2,2},{4,7},{7,4},{5,5},{6,6},{8,11},{11,8},{9,9... | collective-permute-start | bytes 98312 | tf_op jit(solution)/shard_map/ppermute | solution.py:267
  12.5 5.7 %collective-permute-start.1 = (bf16[16,1024]{1,0:T(8,128)(2,1)S(1)}, bf16[16,1024]{1,0:T(8,128)(2,1)S(1)}, u32[]{:S(2)}, u32[]{:S(2)}) collective-permute-start(bf16[16,1024]{1,0:T(8,128)(2,1)S(1)} %get-tuple-element.8.refs_5_), channel_id=1, source_target_pairs={{1,3},{3,1},{0,0},{2,2},{5,7},{7,5},{4,4},{6,6},{9,11},{11,9},{8,8... | collective-permute-start | bytes 98312 | tf_op jit(solution)/shard_map/ppermute | solution.py:267
  13.1 5.0 %collective-permute-start = (bf16[16,1024]{1,0:T(8,128)(2,1)S(1)}, bf16[16,1024]{1,0:T(8,128)(2,1)S(1)}, u32[]{:S(2)}, u32[]{:S(2)}) collective-permute-start(bf16[16,1024]{1,0:T(8,128)(2,1)S(1)} %get-tuple-element.8.refs_5_), channel_id=1, source_target_pairs={{2,3},{3,2},{0,0},{1,1},{6,7},{7,6},{4,4},{5,5},{10,11},{11,10},{8... | collective-permute-start | bytes 98312 | tf_op jit(solution)/shard_map/ppermute | solution.py:267
  18.3 7.5 %collective-permute-start.10 = (bf16[16,4224]{1,0:T(8,128)(2,1)S(1)}, bf16[16,4224]{1,0:T(8,128)(2,1)S(1)}, u32[]{:S(2)}, u32[]{:S(2)}) collective-permute-start(bf16[16,4224]{1,0:T(8,128)(2,1)S(1)} %join.1.rows), channel_id=1, source_target_pairs={{0,24},{4,28},{8,16},{12,20},{16,8},{20,12},{24,0},{28,4},{1,25},{... | collective-permute-start | bytes 405512 | tf_op jit(solution)/shard_map/ppermute | solution.py:258
  21.3 5.5 %collective-permute-start.8 = (bf16[16,4224]{1,0:T(8,128)(2,1)S(1)}, bf16[16,4224]{1,0:T(8,128)(2,1)S(1)}, u32[]{:S(2)}, u32[]{:S(2)}) collective-permute-start(bf16[16,4224]{1,0:T(8,128)(2,1)S(1)} %join.1.rows), channel_id=1, source_target_pairs={{0,16},{4,20},{8,24},{12,28},{16,0},{20,4},{24,8},{28,12},{1,17},{... | collective-permute-start | bytes 405512 | tf_op jit(solution)/shard_map/ppermute | solution.py:258
  21.8 5.0 %collective-permute-start.6 = (bf16[16,4224]{1,0:T(8,128)(2,1)S(1)}, bf16[16,4224]{1,0:T(8,128)(2,1)S(1)}, u32[]{:S(2)}, u32[]{:S(2)}) collective-permute-start(bf16[16,4224]{1,0:T(8,128)(2,1)S(1)} %join.1.rows), channel_id=1, source_target_pairs={{0,8},{4,12},{8,0},{12,4},{16,24},{20,28},{24,16},{28,20},{1,9},{5... | collective-permute-start | bytes 405512 | tf_op jit(solution)/shard_map/ppermute | solution.py:258
  24.1 3.1 %collective-permute-start.5 = (bf16[16,4224]{1,0:T(8,128)(2,1)S(1)}, bf16[16,4224]{1,0:T(8,128)(2,1)S(1)}, u32[]{:S(2)}, u32[]{:S(2)}) collective-permute-start(bf16[16,4224]{1,0:T(8,128)(2,1)S(1)} %get-tuple-element.11.refs_0_), channel_id=1, source_target_pairs={{0,4},{4,0},{8,12},{12,8},{16,20},{20,16},{24,28},{28,24},{1,5},{5... | collective-permute-start | bytes 405512 | tf_op jit(solution)/shard_map/ppermute | solution.py:258
  25.8 1.5 %collective-permute-start.11 = (bf16[16,4224]{1,0:T(8,128)(2,1)S(1)}, bf16[16,4224]{1,0:T(8,128)(2,1)S(1)}, u32[]{:S(2)}, u32[]{:S(2)}) collective-permute-start(bf16[16,4224]{1,0:T(8,128)(2,1)S(1)} %collective-permute-done.10.refs_6_), channel_id=1, source_target_pairs={{0,4},{4,0},{8,12},{12,8},{16,20},{20,16},{24,28},{28,24},{1,5},{5... | collective-permute-start | bytes 405512 | tf_op jit(solution)/shard_map/ppermute | solution.py:258
  26.7 1.4 %collective-permute-start.9 = (bf16[16,4224]{1,0:T(8,128)(2,1)S(1)}, bf16[16,4224]{1,0:T(8,128)(2,1)S(1)}, u32[]{:S(2)}, u32[]{:S(2)}) collective-permute-start(bf16[16,4224]{1,0:T(8,128)(2,1)S(1)} %collective-permute-done.8.refs_4_), channel_id=1, source_target_pairs={{0,4},{4,0},{8,12},{12,8},{16,20},{20,16},{24,28},{28,24},{1,5},{5... | collective-permute-start | bytes 405512 | tf_op jit(solution)/shard_map/ppermute | solution.py:258
  26.8 1.5 %collective-permute-start.7 = (bf16[16,4224]{1,0:T(8,128)(2,1)S(1)}, bf16[16,4224]{1,0:T(8,128)(2,1)S(1)}, u32[]{:S(2)}, u32[]{:S(2)}) collective-permute-start(bf16[16,4224]{1,0:T(8,128)(2,1)S(1)} %collective-permute-done.6.refs_2_), channel_id=1, source_target_pairs={{0,4},{4,0},{8,12},{12,8},{16,20},{20,16},{24,28},{28,24},{1,5},{5... | collective-permute-start | bytes 405512 | tf_op jit(solution)/shard_map/ppermute | solution.py:258

commit v2 on v0

--- a/solution.py
+++ b/solution.py
@@ -13,6 +13,7 @@
 CODE = 128
 DIGIT = 64
 GROUP = 16
+CHUNK = 1024
 
 
 def vmem_limit(mebibytes):
@@ -33,9 +34,9 @@
     copies = [
         pltpu.make_async_copy(offsets, offset, sems.at[0]),
         pltpu.make_async_copy(mask, alive, sems.at[1]),
-        pltpu.make_async_copy(targets, target, sems.at[2]),
-        pltpu.make_async_copy(gain, gain_out, sems.at[3]),
-        pltpu.make_async_copy(hidden.at[0, pl.ds(first, depth)], window, sems.at[4]),
+        pltpu.make_async_copy(hidden.at[0, pl.ds(first, depth)], window, sems.at[2]),
+        pltpu.make_async_copy(targets, target, sems.at[3]),
+        pltpu.make_async_copy(gain, gain_out, sems.at[4]),
     ]
     for copy in copies:
         copy.start()
@@ -55,15 +56,15 @@
     offset_in = (lengths[0] - 1 - first) - offset[...]
     wanted = jnp.sum(chosen * (offset_in + 1).astype(jnp.float32), axis=1, keepdims=True) - 1.0
     select = jnp.where(iota((LIVE, depth), 1).astype(jnp.float32) == wanted, 1.0, 0.0).astype(jnp.bfloat16)
-    copies[2].wait()
+    copies[3].wait()
     ids = jnp.sum(chosen * target[...].astype(jnp.float32), axis=1, keepdims=True).astype(jnp.int32)
     lane = iota((LIVE, CODE), 1)
     digits = jnp.where(
         lane == 0, ids % DIGIT, jnp.where(lane == 1, (ids // DIGIT) % DIGIT, jnp.where(lane == 2, ids // (DIGIT * DIGIT), 0))
     )
     codes[...] = digits.astype(jnp.float32).astype(jnp.bfloat16)
-    for copy in copies[3:]:
-        copy.wait()
+    copies[4].wait()
+    copies[2].wait()
     rows[...] = jnp.dot(select, window[...], preferred_element_type=jnp.float32).astype(jnp.bfloat16)
 
 
@@ -151,8 +152,8 @@
     )(in_hbm(head), rows)
 
 
-def score_kernel(*refs):
-    dp = len(refs) - 2
+def score_kernel(order, *refs):
+    dp = len(order)
     pieces, (head, stats) = refs[:dp], refs[dp:]
     depth, vocab_width = head.shape
     live = pieces[0].shape[0]
@@ -160,8 +161,10 @@
     mine = lax.axis_index("dp")
     start = (mine * stats.shape[1] + lax.axis_index("tensor")) * vocab_width
 
-    normed = jnp.concatenate([piece[:, :depth] for piece in pieces], axis=0)
-    logits = jnp.dot(normed, head[...], preferred_element_type=jnp.float32)
+    logits = jnp.zeros((row_count, vocab_width), jnp.float32)
+    for k in range(0, depth, CHUNK):
+        normed = jnp.concatenate([piece[:, k : k + CHUNK] for piece in pieces], axis=0)
+        logits += jnp.dot(normed, head[k : k + CHUNK], preferred_element_type=jnp.float32)
     digits = jnp.concatenate([piece[:, depth:] for piece in pieces], axis=0).astype(jnp.float32)
     lane = lax.broadcasted_iota(jnp.int32, (row_count, CODE), 1)
     weight = jnp.where(lane == 0, 1.0, jnp.where(lane == 1, float(DIGIT), jnp.where(lane == 2, float(DIGIT * DIGIT), 0.0)))
@@ -173,22 +176,23 @@
     weighted = jnp.sum(expo * logits, axis=-1, keepdims=True)
     chosen = jnp.sum(jnp.where(column == target, logits, 0.0), axis=-1, keepdims=True)
     spot = lane - lax.broadcasted_iota(jnp.int32, (row_count, CODE), 0) % live
-    table = jnp.zeros((row_count, CODE), jnp.float32)
-    for group, value in enumerate((top, total, weighted, chosen)):
-        table = jnp.where(spot == GROUP * group, value, table)
-    for d in range(dp):
-        line = jnp.sum(table[d * live : (d + 1) * live], axis=0, keepdims=True)
-        for t in range(stats.shape[1]):
-            stats[mine ^ d, t] = line
-
-
-def score(pieces, head, copies):
-    dp = len(pieces)
-    live, width = pieces[0].shape
-    vmem = pl.BlockSpec(memory_space=pltpu.VMEM)
-    return pl.pallas_call(
-        score_kernel,
-        out_shape=jax.ShapeDtypeStruct((dp, copies, 1, CODE), jnp.float32),
+    tops = jnp.where((spot == 0) | (spot == GROUP), top, 0.0)
+    sums = jnp.zeros((row_count, CODE), jnp.float32)
+    for group, value in enumerate((total, weighted, chosen)):
+        sums = jnp.where(spot == GROUP * group, value, sums)
+    for i, d in enumerate(order):
+        for line, table in enumerate((tops, sums)):
+            packed = jnp.sum(table[i * live : (i + 1) * live], axis=0, keepdims=True)
+            for t in range(stats.shape[1]):
+                stats[mine ^ d, t, line : line + 1] = packed
+
+
+def score(pieces, order, head, copies):
+    dp = len(order)
+    vmem = pl.BlockSpec(memory_space=pltpu.VMEM)
+    return pl.pallas_call(
+        functools.partial(score_kernel, order),
+        out_shape=jax.ShapeDtypeStruct((dp, copies, 2, CODE), jnp.float32),
         in_specs=[vmem] * (dp + 1),
         out_specs=vmem,
         compiler_params=vmem_limit(32),
@@ -196,21 +200,12 @@
     )(*pieces, pltpu.with_memory_space_constraint(head, pltpu.VMEM))
 
 
-def combine(values):
-    lane = lax.broadcasted_iota(jnp.int32, values.shape, 1)
-    top = jnp.where(lane < GROUP, values, 0.0)
-    top = top + pltpu.roll(top, GROUP, 1)
-    top = top + pltpu.roll(top, 2 * GROUP, 1)
-    best = jnp.max(top, axis=0, keepdims=True)
-    factor = jnp.where(lane < 3 * GROUP, jnp.exp(top - best), 1.0)
-    return jnp.sum(values * factor, axis=0, keepdims=True), best
-
-
 def finish_kernel(stats, place, logprob, entropy, scored, spread, sems):
-    sums, best = combine(stats[:, 0, :])
-    total = pltpu.roll(sums, CODE - GROUP, 1)
-    weighted = pltpu.roll(sums, CODE - 2 * GROUP, 1)
-    chosen = pltpu.roll(sums, CODE - 3 * GROUP, 1)
+    tops = stats[:, 0:1, :]
+    best = jnp.max(tops, axis=0)
+    total = jnp.sum(stats[:, 1:2, :] * jnp.exp(tops - best), axis=0)
+    weighted = pltpu.roll(total, CODE - GROUP, 1)
+    chosen = pltpu.roll(total, CODE - 2 * GROUP, 1)
     lse = best + jnp.log(total)
     lane = lax.broadcasted_iota(jnp.int32, (LIVE, CODE), 1)
     row = lax.broadcasted_iota(jnp.int32, (LIVE, CODE), 0)
@@ -261,8 +256,9 @@
     held, pieces[0] = fetch(head, rows)
     for d in range(0, dp, 2):
         pieces[d + 1] = swap(pieces[d], "dp", 1)
-    stats = score([pieces[d] for d in range(dp)], held, tensor)
-    stats = lax.all_to_all(stats.reshape(dp * tensor, 1, CODE), ("dp", "tensor"), 0, 0, tiled=True)
+    order = [0, 1] + [d + core for d in reversed(range(2, dp, 2)) for core in (0, 1)]
+    stats = score([pieces[d] for d in order], order, held, tensor)
+    stats = lax.all_to_all(stats.reshape(dp * tensor, 2, CODE), ("dp", "tensor"), 0, 0, tiled=True)
     return finish(stats, slots, offsets.shape[1])
 
 

time: 34.6 us -> 35.1 us (1.014)
  waiting for transfers between devices: 7.55 us -> 8.68 us
  starting transfers between devices: 9.89 us -> 9.39 us
    ppermute x10, waiting for transfers between devices: 7.55 us -> 8.68 us  [swap(): lax.ppermute(x, axis, [(i, i ^ distance) for i in range(lax.axis_size(axi...]
    ppermute x10, starting transfers between devices: 9.89 us -> 9.39 us  [swap(): lax.ppermute(x, axis, [(i, i ^ distance) for i in range(lax.axis_size(axi...]
  transfers between devices with their start and end apart: 10 -> 10, of which waited for: 7 -> 6; matrix products, arithmetic and copies ran while one was open for 0% -> 0% of each run, Pallas kernels for 6% -> 6%
where the time goes in v2:
time: 35.1 us; the launch traced here: 34.9 us
  blocking collectives  10.1 us (29%)
  starting transfers between devices  9.39 us (27%)
  waiting for transfers between devices  8.68 us (25%)
  Pallas kernels  5.32 us (15%)
  between operations  1.33 us (4%)
    all_to_all x1, blocking collectives, per_device(): lax.all_to_all(stats.reshape(dp * tensor, 2, CODE), ('dp', 'tensor'), 0,...  10.1 us
    ppermute x10, starting transfers between devices, swap(): lax.ppermute(x, axis, [(i, i ^ distance) for i in range(lax.axis_size(axi...  9.39 us
    ppermute x10, waiting for transfers between devices, swap(): lax.ppermute(x, axis, [(i, i ^ distance) for i in range(lax.axis_size(axi...  8.68 us
    pallas_call x1, Pallas kernels, fetch(): pl.pallas_call(fetch_kernel, out_shape=(pltpu.VMEM(head.shape, head.dtype...  2.21 us
    pallas_call x1, Pallas kernels, pick(): pl.pallas_call(pick_kernel, out_shape=(jax.ShapeDtypeStruct((LIVE, featur...  1.34 us
    pallas_call x1, Pallas kernels, score(): pl.pallas_call(functools.partial(score_kernel, order), out_shape=jax.Shap...  0.9 us
    pallas_call x1, Pallas kernels, finish(): pl.pallas_call(finish_kernel, out_shape=(out, out), in_specs=[vmem, vmem]...  0.75 us
  transfers between devices with their start and end apart: 10, of which 6 were waited for; matrix products, arithmetic and copies ran while one was open for 0% of the time, Pallas kernels for 6%

profile of v2, /device:TPU:0, one launch (start us, length us, event | category | flops | bytes accessed | tf_op | source)
XLA Modules:
  0.0 34.9 jit_solution(15537463596074098062)
XLA Ops:
  1.3 1.3 %pick.1 = (bf16[16,1024]{1,0:T(8,128)(2,1)S(1)}, bf16[16,128]{1,0:T(8,128)(2,1)S(1)}, f32[16,32]{1,0:T(8,128)S(1)}, f32[1,4096]{1,0:T(1,128)S(1)}) custom-call(s32[1]{0:T(128)S(6)} %copy.9.lengths, s32[1,32]{1,0:T(1,128)} %offsets.1, s32[1,32]{1,0:T(1,128)} %targets.1, s32[1,32]{1,0:T(1,128)} %mask.1, f32[1,4096]{1,0:T(1,128)} %bitcast.3, ...), custom_call_target="tpu_custom_call" | custom-call | tf_op jit(solution)/shard_map/pick/pallas_call | solution.py:75
  2.6 5.1 %collective-permute-start.2 = (bf16[16,1024]{1,0:T(8,128)(2,1)S(1)}, bf16[16,1024]{1,0:T(8,128)(2,1)S(1)}, u32[]{:S(2)}, u32[]{:S(2)}) collective-permute-start(bf16[16,1024]{1,0:T(8,128)(2,1)S(1)} %get-tuple-element.8.refs_0_), channel_id=1, source_target_pairs={{0,3},{1,2},{2,1},{3,0},{4,7},{5,6},{6,5},{7,4},{8,11},{9,10},{10,... | collective-permute-start | bytes 98312 | tf_op jit(solution)/shard_map/ppermute | solution.py:246
  7.7 0.0 collective-permute-start.1
  7.7 0.6 %collective-permute-start = (bf16[16,1024]{1,0:T(8,128)(2,1)S(1)}, bf16[16,1024]{1,0:T(8,128)(2,1)S(1)}, u32[]{:S(2)}, u32[]{:S(2)}) collective-permute-start(bf16[16,1024]{1,0:T(8,128)(2,1)S(1)} %get-tuple-element.8.refs_0_), channel_id=1, source_target_pairs={{0,1},{1,0},{2,3},{3,2},{4,5},{5,4},{6,7},{7,6},{8,9},{9,8},{10,11... | collective-permute-start | bytes 98312 | tf_op jit(solution)/shard_map/ppermute | solution.py:246
  8.4 1.3 %collective-permute-done.2.refs_3_ = bf16[16,1024]{1,0:T(8,128)(2,1)S(1)} collective-permute-done((bf16[16,1024]{1,0:T(8,128)(2,1)S(1)}, bf16[16,1024]{1,0:T(8,128)(2,1)S(1)}, u32[]{:S(2)}, u32[]{:S(2)}) %collective-permute-start.2) | collective-permute-done | bytes 32800 | tf_op jit(solution)/shard_map/ppermute | solution.py:246
  9.6 2.9 %collective-permute-done.1.refs_2_ = bf16[16,1024]{1,0:T(8,128)(2,1)S(1)} collective-permute-done((bf16[16,1024]{1,0:T(8,128)(2,1)S(1)}, bf16[16,1024]{1,0:T(8,128)(2,1)S(1)}, u32[]{:S(2)}, u32[]{:S(2)}) %collective-permute-start.1) | collective-permute-done | bytes 32800 | tf_op jit(solution)/shard_map/ppermute | solution.py:246
  12.6 0.0 collective-permute-done.refs_1_
  12.6 0.1 join.1.rows
  12.7 1.6 %collective-permute-start.8 = (bf16[16,4224]{1,0:T(8,128)(2,1)S(1)}, bf16[16,4224]{1,0:T(8,128)(2,1)S(1)}, u32[]{:S(2)}, u32[]{:S(2)}) collective-permute-start(bf16[16,4224]{1,0:T(8,128)(2,1)S(1)} %join.1.rows), channel_id=1, source_target_pairs={{0,8},{4,12},{8,0},{12,4},{16,24},{20,28},{24,16},{28,20},{1,9},{5... | collective-permute-start | bytes 405512 | tf_op jit(solution)/shard_map/ppermute | solution.py:246
  14.3 1.5 %collective-permute-start.6 = (bf16[16,4224]{1,0:T(8,128)(2,1)S(1)}, bf16[16,4224]{1,0:T(8,128)(2,1)S(1)}, u32[]{:S(2)}, u32[]{:S(2)}) collective-permute-start(bf16[16,4224]{1,0:T(8,128)(2,1)S(1)} %join.1.rows), channel_id=1, source_target_pairs={{0,16},{4,20},{8,24},{12,28},{16,0},{20,4},{24,8},{28,12},{1,17},{... | collective-permute-start | bytes 405512 | tf_op jit(solution)/shard_map/ppermute | solution.py:246
  15.8 0.5 %collective-permute-start.4 = (bf16[16,4224]{1,0:T(8,128)(2,1)S(1)}, bf16[16,4224]{1,0:T(8,128)(2,1)S(1)}, u32[]{:S(2)}, u32[]{:S(2)}) collective-permute-start(bf16[16,4224]{1,0:T(8,128)(2,1)S(1)} %join.1.rows), channel_id=1, source_target_pairs={{0,24},{4,28},{8,16},{12,20},{16,8},{20,12},{24,0},{28,4},{1,25},{... | collective-permute-start | bytes 405512 | tf_op jit(solution)/shard_map/ppermute | solution.py:246
  16.2 2.2 %fetch.1 = (bf16[4096,512]{1,0:T(8,128)(2,1)S(1)}, bf16[16,4224]{1,0:T(8,128)(2,1)S(1)}) custom-call(bf16[4096,512]{1,0:T(8,128)(2,1)} %head.1, bf16[16,4224]{1,0:T(8,128)(2,1)S(1)} %join.1.rows), custom_call_target="tpu_custom_call" | custom-call | bytes 8388608 | tf_op jit(solution)/shard_map/fetch/pallas_call | solution.py:143
  18.5 0.1 collective-permute-start.3
  18.5 0.5 %collective-permute-done.8.refs_6_ = bf16[16,4224]{1,0:T(8,128)(2,1)S(1)} collective-permute-done((bf16[16,4224]{1,0:T(8,128)(2,1)S(1)}, bf16[16,4224]{1,0:T(8,128)(2,1)S(1)}, u32[]{:S(2)}, u32[]{:S(2)}) %collective-permute-start.8) | collective-permute-done | bytes 135200 | tf_op jit(solution)/shard_map/ppermute | solution.py:246
  19.1 0.0 collective-permute-start.9
  19.1 1.2 %collective-permute-done.6.refs_4_ = bf16[16,4224]{1,0:T(8,128)(2,1)S(1)} collective-permute-done((bf16[16,4224]{1,0:T(8,128)(2,1)S(1)}, bf16[16,4224]{1,0:T(8,128)(2,1)S(1)}, u32[]{:S(2)}, u32[]{:S(2)}) %collective-permute-start.6) | collective-permute-done | bytes 135200 | tf_op jit(solution)/shard_map/ppermute | solution.py:246
  20.3 0.0 collective-permute-start.7
  20.3 1.4 %collective-permute-done.4.refs_2_ = bf16[16,4224]{1,0:T(8,128)(2,1)S(1)} collective-permute-done((bf16[16,4224]{1,0:T(8,128)(2,1)S(1)}, bf16[16,4224]{1,0:T(8,128)(2,1)S(1)}, u32[]{:S(2)}, u32[]{:S(2)}) %collective-permute-start.4) | collective-permute-done | bytes 135200 | tf_op jit(solution)/shard_map/ppermute | solution.py:246
  21.7 0.0 collective-permute-start.5
  21.7 0.0 collective-permute-done.3.refs_1_
  21.7 0.0 collective-permute-done.9.refs_7_
  21.7 0.0 collective-permute-done.7.refs_5_
  21.7 1.3 %collective-permute-done.5.refs_3_ = bf16[16,4224]{1,0:T(8,128)(2,1)S(1)} collective-permute-done((bf16[16,4224]{1,0:T(8,128)(2,1)S(1)}, bf16[16,4224]{1,0:T(8,128)(2,1)S(1)}, u32[]{:S(2)}, u32[]{:S(2)}) %collective-permute-start.5) | collective-permute-done | bytes 135200 | tf_op jit(solution)/shard_map/ppermute | solution.py:246
  23.1 0.9 %score.1 = f32[8,4,2,128]{3,2,1,0:T(2,128)S(1)} custom-call(bf16[16,4224]{1,0:T(8,128)(2,1)S(1)} %get-tuple-element.11.refs_0_, bf16[16,4224]{1,0:T(8,128)(2,1)S(1)} %collective-permute-done.3.refs_1_, bf16[16,4224]{1,0:T(8,128)(2,1)S(1)} %collective-permute-done.4.refs_2_, bf16[16,4224]{1,0:T(8,128)(2,1)S(1)} %collective-permute-done.5.refs_3_, ...), custom_call_target="tpu_custom_call" | custom-call | tf_op jit(solution)/shard_map/score/pallas_call | solution.py:193
  24.0 10.1 %all_to_all.5.stats = f32[32,2,128]{2,1,0:T(2,128)S(1)} all-to-all(f32[32,2,128]{2,1,0:T(2,128)S(1)} %bitcast.2), channel_id=1, replica_groups=mesh['dp'=8,'tensor'=4] {'dp','tensor'}, dimensions={0} | all-to-all | bytes 65536 | tf_op jit(solution)/shard_map/all_to_all | solution.py:261
  34.1 0.7 %finish.1 = (f32[1,32]{1,0:T(1,128)}, f32[1,32]{1,0:T(1,128)}) custom-call(f32[32,2,128]{2,1,0:T(2,128)S(1)} %all_to_all.5.stats, f32[16,32]{1,0:T(8,128)S(1)} %get-tuple-element.13.place), custom_call_target="tpu_custom_call" | custom-call | tf_op jit(solution)/shard_map/finish/pallas_call | solution.py:230
Async XLA Ops:
  2.6 7.0 %collective-permute-start.2 = (bf16[16,1024]{1,0:T(8,128)(2,1)S(1)}, bf16[16,1024]{1,0:T(8,128)(2,1)S(1)}, u32[]{:S(2)}, u32[]{:S(2)}) collective-permute-start(bf16[16,1024]{1,0:T(8,128)(2,1)S(1)} %get-tuple-element.8.refs_0_), channel_id=1, source_target_pairs={{0,3},{1,2},{2,1},{3,0},{4,7},{5,6},{6,5},{7,4},{8,11},{9,10},{10,... | collective-permute-start | bytes 98312 | tf_op jit(solution)/shard_map/ppermute | solution.py:246
  7.7 4.8 %collective-permute-start.1 = (bf16[16,1024]{1,0:T(8,128)(2,1)S(1)}, bf16[16,1024]{1,0:T(8,128)(2,1)S(1)}, u32[]{:S(2)}, u32[]{:S(2)}) collective-permute-start(bf16[16,1024]{1,0:T(8,128)(2,1)S(1)} %get-tuple-element.8.refs_0_), channel_id=1, source_target_pairs={{0,2},{1,3},{2,0},{3,1},{4,6},{5,7},{6,4},{7,5},{8,10},{9,11},{10,... | collective-permute-start | bytes 98312 | tf_op jit(solution)/shard_map/ppermute | solution.py:246
  7.7 4.8 %collective-permute-start = (bf16[16,1024]{1,0:T(8,128)(2,1)S(1)}, bf16[16,1024]{1,0:T(8,128)(2,1)S(1)}, u32[]{:S(2)}, u32[]{:S(2)}) collective-permute-start(bf16[16,1024]{1,0:T(8,128)(2,1)S(1)} %get-tuple-element.8.refs_0_), channel_id=1, source_target_pairs={{0,1},{1,0},{2,3},{3,2},{4,5},{5,4},{6,7},{7,6},{8,9},{9,8},{10,11... | collective-permute-start | bytes 98312 | tf_op jit(solution)/shard_map/ppermute | solution.py:246
  12.7 6.4 %collective-permute-start.8 = (bf16[16,4224]{1,0:T(8,128)(2,1)S(1)}, bf16[16,4224]{1,0:T(8,128)(2,1)S(1)}, u32[]{:S(2)}, u32[]{:S(2)}) collective-permute-start(bf16[16,4224]{1,0:T(8,128)(2,1)S(1)} %join.1.rows), channel_id=1, source_target_pairs={{0,8},{4,12},{8,0},{12,4},{16,24},{20,28},{24,16},{28,20},{1,9},{5... | collective-permute-start | bytes 405512 | tf_op jit(solution)/shard_map/ppermute | solution.py:246
  14.3 6.0 %collective-permute-start.6 = (bf16[16,4224]{1,0:T(8,128)(2,1)S(1)}, bf16[16,4224]{1,0:T(8,128)(2,1)S(1)}, u32[]{:S(2)}, u32[]{:S(2)}) collective-permute-start(bf16[16,4224]{1,0:T(8,128)(2,1)S(1)} %join.1.rows), channel_id=1, source_target_pairs={{0,16},{4,20},{8,24},{12,28},{16,0},{20,4},{24,8},{28,12},{1,17},{... | collective-permute-start | bytes 405512 | tf_op jit(solution)/shard_map/ppermute | solution.py:246
  15.8 6.0 %collective-permute-start.4 = (bf16[16,4224]{1,0:T(8,128)(2,1)S(1)}, bf16[16,4224]{1,0:T(8,128)(2,1)S(1)}, u32[]{:S(2)}, u32[]{:S(2)}) collective-permute-start(bf16[16,4224]{1,0:T(8,128)(2,1)S(1)} %join.1.rows), channel_id=1, source_target_pairs={{0,24},{4,28},{8,16},{12,20},{16,8},{20,12},{24,0},{28,4},{1,25},{... | collective-permute-start | bytes 405512 | tf_op jit(solution)/shard_map/ppermute | solution.py:246
  18.5 3.3 %collective-permute-start.3 = (bf16[16,4224]{1,0:T(8,128)(2,1)S(1)}, bf16[16,4224]{1,0:T(8,128)(2,1)S(1)}, u32[]{:S(2)}, u32[]{:S(2)}) collective-permute-start(bf16[16,4224]{1,0:T(8,128)(2,1)S(1)} %get-tuple-element.11.refs_0_), channel_id=1, source_target_pairs={{0,4},{4,0},{8,12},{12,8},{16,20},{20,16},{24,28},{28,24},{1,5},{5... | collective-permute-start | bytes 405512 | tf_op jit(solution)/shard_map/ppermute | solution.py:246
  19.1 2.7 %collective-permute-start.9 = (bf16[16,4224]{1,0:T(8,128)(2,1)S(1)}, bf16[16,4224]{1,0:T(8,128)(2,1)S(1)}, u32[]{:S(2)}, u32[]{:S(2)}) collective-permute-start(bf16[16,4224]{1,0:T(8,128)(2,1)S(1)} %collective-permute-done.8.refs_6_), channel_id=1, source_target_pairs={{0,4},{4,0},{8,12},{12,8},{16,20},{20,16},{24,28},{28,24},{1,5},{5... | collective-permute-start | bytes 405512 | tf_op jit(solution)/shard_map/ppermute | solution.py:246
  20.3 1.5 %collective-permute-start.7 = (bf16[16,4224]{1,0:T(8,128)(2,1)S(1)}, bf16[16,4224]{1,0:T(8,128)(2,1)S(1)}, u32[]{:S(2)}, u32[]{:S(2)}) collective-permute-start(bf16[16,4224]{1,0:T(8,128)(2,1)S(1)} %collective-permute-done.6.refs_4_), channel_id=1, source_target_pairs={{0,4},{4,0},{8,12},{12,8},{16,20},{20,16},{24,28},{28,24},{1,5},{5... | collective-permute-start | bytes 405512 | tf_op jit(solution)/shard_map/ppermute | solution.py:246
  21.7 1.4 %collective-permute-start.5 = (bf16[16,4224]{1,0:T(8,128)(2,1)S(1)}, bf16[16,4224]{1,0:T(8,128)(2,1)S(1)}, u32[]{:S(2)}, u32[]{:S(2)}) collective-permute-start(bf16[16,4224]{1,0:T(8,128)(2,1)S(1)} %collective-permute-done.4.refs_2_), channel_id=1, source_target_pairs={{0,4},{4,0},{8,12},{12,8},{16,20},{20,16},{24,28},{28,24},{1,5},{5... | collective-permute-start | bytes 405512 | tf_op jit(solution)/shard_map/ppermute | solution.py:246

commit v3 on v2

--- a/solution.py
+++ b/solution.py
@@ -13,7 +13,6 @@
 CODE = 128
 DIGIT = 64
 GROUP = 16
-CHUNK = 1024
 
 
 def vmem_limit(mebibytes):
@@ -104,7 +103,7 @@
         square += jnp.sum(values * values, axis=-1, keepdims=True)
     scale = lax.rsqrt(square / (tensor * features) + 1e-06)
     shard = lax.axis_index("tensor")
-    for s, part in enumerate(parts):
+    for s, part in enumerate(reversed(parts)):
         span = pl.ds(pl.multiple_of((shard ^ s) * features, features), features)
         rows[:, span] = (part[...].astype(jnp.float32) * scale * gain[:, span]).astype(jnp.bfloat16)
     rows[:, tensor * features :] = codes[...]
@@ -152,19 +151,16 @@
     )(in_hbm(head), rows)
 
 
-def score_kernel(order, *refs):
-    dp = len(order)
-    pieces, (head, stats) = refs[:dp], refs[dp:]
+def score_kernel(order, head, *refs):
+    pieces, (*earlier, stats) = refs[: len(order)], refs[len(order) :]
     depth, vocab_width = head.shape
     live = pieces[0].shape[0]
-    row_count = dp * live
+    row_count = len(order) * live
     mine = lax.axis_index("dp")
-    start = (mine * stats.shape[1] + lax.axis_index("tensor")) * vocab_width
-
-    logits = jnp.zeros((row_count, vocab_width), jnp.float32)
-    for k in range(0, depth, CHUNK):
-        normed = jnp.concatenate([piece[:, k : k + CHUNK] for piece in pieces], axis=0)
-        logits += jnp.dot(normed, head[k : k + CHUNK], preferred_element_type=jnp.float32)
+    start = (mine * lax.axis_size("tensor") + lax.axis_index("tensor")) * vocab_width
+
+    normed = jnp.concatenate([piece[:, :depth] for piece in pieces], axis=0)
+    logits = jnp.dot(normed, head[...], preferred_element_type=jnp.float32)
     digits = jnp.concatenate([piece[:, depth:] for piece in pieces], axis=0).astype(jnp.float32)
     lane = lax.broadcasted_iota(jnp.int32, (row_count, CODE), 1)
     weight = jnp.where(lane == 0, 1.0, jnp.where(lane == 1, float(DIGIT), jnp.where(lane == 2, float(DIGIT * DIGIT), 0.0)))
@@ -183,21 +179,26 @@
     for i, d in enumerate(order):
         for line, table in enumerate((tops, sums)):
             packed = jnp.sum(table[i * live : (i + 1) * live], axis=0, keepdims=True)
-            for t in range(stats.shape[1]):
-                stats[mine ^ d, t, line : line + 1] = packed
-
-
-def score(pieces, order, head, copies):
-    dp = len(order)
+            if earlier:
+                for t in range(stats.shape[1]):
+                    stats[mine ^ d, t, line : line + 1] = packed
+            else:
+                stats[i, line : line + 1] = packed
+    for i, d in enumerate(order if earlier else ()):
+        for t in range(stats.shape[1]):
+            stats[mine ^ (d - 1), t] = earlier[0][i]
+
+
+def score(order, head, pieces, *rest, shape):
     vmem = pl.BlockSpec(memory_space=pltpu.VMEM)
     return pl.pallas_call(
         functools.partial(score_kernel, order),
-        out_shape=jax.ShapeDtypeStruct((dp, copies, 2, CODE), jnp.float32),
-        in_specs=[vmem] * (dp + 1),
+        out_shape=jax.ShapeDtypeStruct(shape, jnp.float32),
+        in_specs=[vmem] * (1 + len(order) + len(rest)),
         out_specs=vmem,
         compiler_params=vmem_limit(32),
         name="score",
-    )(*pieces, pltpu.with_memory_space_constraint(head, pltpu.VMEM))
+    )(pltpu.with_memory_space_constraint(head, pltpu.VMEM), *[pieces[d] for d in order], *rest)
 
 
 def finish_kernel(stats, place, logprob, entropy, scored, spread, sems):
@@ -250,14 +251,14 @@
     dp, tensor = lax.axis_size("dp"), lax.axis_size("tensor")
     rows, codes, slots, gain = pick(hidden, gain, lengths, offsets, targets, mask)
     parts = {0: rows} | {s: swap(rows, "tensor", s) for s in reversed(range(1, tensor))}
-    rows = join([parts[s] for s in range(tensor)], codes, gain)
+    rows = join([parts[s] for s in reversed(range(tensor))], codes, gain)
 
     pieces = {d: swap(rows, "dp", d) for d in reversed(range(2, dp, 2))}
     held, pieces[0] = fetch(head, rows)
     for d in range(0, dp, 2):
         pieces[d + 1] = swap(pieces[d], "dp", 1)
-    order = [0, 1] + [d + core for d in reversed(range(2, dp, 2)) for core in (0, 1)]
-    stats = score([pieces[d] for d in order], order, held, tensor)
+    early = score(range(dp - 2, -1, -2), held, pieces, shape=(dp // 2, 2, CODE))
+    stats = score(range(dp - 1, 0, -2), held, pieces, early, shape=(dp, tensor, 2, CODE))
     stats = lax.all_to_all(stats.reshape(dp * tensor, 2, CODE), ("dp", "tensor"), 0, 0, tiled=True)
     return finish(stats, slots, offsets.shape[1])
 

time: 35.1 us -> 34.8 us (level)
  waiting for transfers between devices: 8.68 us -> 6.53 us
  Pallas kernels: 5.32 us -> 6.49 us
  starting transfers between devices: 9.39 us -> 9.89 us
    ppermute x10, waiting for transfers between devices: 8.68 us -> 6.53 us  [swap(): lax.ppermute(x, axis, [(i, i ^ distance) for i in range(lax.axis_size(axi...]
    pallas_call x1 -> x2, Pallas kernels: 0.9 us -> 2.07 us  [score(): pl.pallas_call(functools.partial(score_kernel, order), out_shape=jax.Shap...]
    ppermute x10, starting transfers between devices: 9.39 us -> 9.89 us  [swap(): lax.ppermute(x, axis, [(i, i ^ distance) for i in range(lax.axis_size(axi...]
  transfers between devices with their start and end apart: 10 -> 10, of which waited for: 6 -> 4; matrix products, arithmetic and copies ran while one was open for 0% -> 0% of each run, Pallas kernels for 6% -> 9%
where the time goes in v3:
time: 34.8 us; the launch traced here: 34.5 us
  blocking collectives  10.2 us (29%)
  starting transfers between devices  9.89 us (28%)
  waiting for transfers between devices  6.53 us (19%)
  Pallas kernels  6.49 us (19%)
  between operations  1.36 us (4%)
    all_to_all x1, blocking collectives, per_device(): lax.all_to_all(stats.reshape(dp * tensor, 2, CODE), ('dp', 'tensor'), 0,...  10.2 us
    ppermute x10, starting transfers between devices, swap(): lax.ppermute(x, axis, [(i, i ^ distance) for i in range(lax.axis_size(axi...  9.89 us
    ppermute x10, waiting for transfers between devices, swap(): lax.ppermute(x, axis, [(i, i ^ distance) for i in range(lax.axis_size(axi...  6.53 us
    pallas_call x1, Pallas kernels, fetch(): pl.pallas_call(fetch_kernel, out_shape=(pltpu.VMEM(head.shape, head.dtype...  2.21 us
    pallas_call x2, Pallas kernels, score(): pl.pallas_call(functools.partial(score_kernel, order), out_shape=jax.Shap...  2.07 us
    pallas_call x1, Pallas kernels, pick(): pl.pallas_call(pick_kernel, out_shape=(jax.ShapeDtypeStruct((LIVE, featur...  1.34 us
    pallas_call x1, Pallas kernels, finish(): pl.pallas_call(finish_kernel, out_shape=(out, out), in_specs=[vmem, vmem]...  0.75 us
  transfers between devices with their start and end apart: 10, of which 4 were waited for; matrix products, arithmetic and copies ran while one was open for 0% of the time, Pallas kernels for 9%

profile of v3, /device:TPU:0, one launch (start us, length us, event | category | flops | bytes accessed | tf_op | source)
XLA Modules:
  0.0 34.5 jit_solution(6724252753998376348)
XLA Ops:
  1.3 1.3 %pick.1 = (bf16[16,1024]{1,0:T(8,128)(2,1)S(1)}, bf16[16,128]{1,0:T(8,128)(2,1)S(1)}, f32[16,32]{1,0:T(8,128)S(1)}, f32[1,4096]{1,0:T(1,128)S(1)}) custom-call(s32[1]{0:T(128)S(6)} %copy.9.lengths, s32[1,32]{1,0:T(1,128)} %offsets.1, s32[1,32]{1,0:T(1,128)} %targets.1, s32[1,32]{1,0:T(1,128)} %mask.1, f32[1,4096]{1,0:T(1,128)} %bitcast.3, ...), custom_call_target="tpu_custom_call" | custom-call | tf_op jit(solution)/shard_map/pick/pallas_call | solution.py:74
  2.6 5.1 %collective-permute-start = (bf16[16,1024]{1,0:T(8,128)(2,1)S(1)}, bf16[16,1024]{1,0:T(8,128)(2,1)S(1)}, u32[]{:S(2)}, u32[]{:S(2)}) collective-permute-start(bf16[16,1024]{1,0:T(8,128)(2,1)S(1)} %get-tuple-element.8.refs_3_), channel_id=1, source_target_pairs={{0,3},{1,2},{2,1},{3,0},{4,7},{5,6},{6,5},{7,4},{8,11},{9,10},{10,... | collective-permute-start | bytes 98312 | tf_op jit(solution)/shard_map/ppermute | solution.py:247
  7.7 0.0 collective-permute-start.1
  7.7 0.6 %collective-permute-start.2 = (bf16[16,1024]{1,0:T(8,128)(2,1)S(1)}, bf16[16,1024]{1,0:T(8,128)(2,1)S(1)}, u32[]{:S(2)}, u32[]{:S(2)}) collective-permute-start(bf16[16,1024]{1,0:T(8,128)(2,1)S(1)} %get-tuple-element.8.refs_3_), channel_id=1, source_target_pairs={{0,1},{1,0},{2,3},{3,2},{4,5},{5,4},{6,7},{7,6},{8,9},{9,8},{10,11... | collective-permute-start | bytes 98312 | tf_op jit(solution)/shard_map/ppermute | solution.py:247
  8.4 1.3 %collective-permute-done.refs_0_ = bf16[16,1024]{1,0:T(8,128)(2,1)S(1)} collective-permute-done((bf16[16,1024]{1,0:T(8,128)(2,1)S(1)}, bf16[16,1024]{1,0:T(8,128)(2,1)S(1)}, u32[]{:S(2)}, u32[]{:S(2)}) %collective-permute-start) | collective-permute-done | bytes 32800 | tf_op jit(solution)/shard_map/ppermute | solution.py:247
  9.6 2.9 %collective-permute-done.1.refs_1_ = bf16[16,1024]{1,0:T(8,128)(2,1)S(1)} collective-permute-done((bf16[16,1024]{1,0:T(8,128)(2,1)S(1)}, bf16[16,1024]{1,0:T(8,128)(2,1)S(1)}, u32[]{:S(2)}, u32[]{:S(2)}) %collective-permute-start.1) | collective-permute-done | bytes 32800 | tf_op jit(solution)/shard_map/ppermute | solution.py:247
  12.6 0.0 collective-permute-done.2.refs_2_
  12.6 0.1 join.1.rows
  12.7 2.5 %collective-permute-start.3 = (bf16[16,4224]{1,0:T(8,128)(2,1)S(1)}, bf16[16,4224]{1,0:T(8,128)(2,1)S(1)}, u32[]{:S(2)}, u32[]{:S(2)}) collective-permute-start(bf16[16,4224]{1,0:T(8,128)(2,1)S(1)} %join.1.rows), channel_id=1, source_target_pairs={{0,24},{4,28},{8,16},{12,20},{16,8},{20,12},{24,0},{28,4},{1,25},{... | collective-permute-start | bytes 405512 | tf_op jit(solution)/shard_map/ppermute | solution.py:247
  15.2 0.5 %collective-permute-start.5 = (bf16[16,4224]{1,0:T(8,128)(2,1)S(1)}, bf16[16,4224]{1,0:T(8,128)(2,1)S(1)}, u32[]{:S(2)}, u32[]{:S(2)}) collective-permute-start(bf16[16,4224]{1,0:T(8,128)(2,1)S(1)} %join.1.rows), channel_id=1, source_target_pairs={{0,16},{4,20},{8,24},{12,28},{16,0},{20,4},{24,8},{28,12},{1,17},{... | collective-permute-start | bytes 405512 | tf_op jit(solution)/shard_map/ppermute | solution.py:247
  15.7 0.5 %collective-permute-start.7 = (bf16[16,4224]{1,0:T(8,128)(2,1)S(1)}, bf16[16,4224]{1,0:T(8,128)(2,1)S(1)}, u32[]{:S(2)}, u32[]{:S(2)}) collective-permute-start(bf16[16,4224]{1,0:T(8,128)(2,1)S(1)} %join.1.rows), channel_id=1, source_target_pairs={{0,8},{4,12},{8,0},{12,4},{16,24},{20,28},{24,16},{28,20},{1,9},{5... | collective-permute-start | bytes 405512 | tf_op jit(solution)/shard_map/ppermute | solution.py:247
  16.3 2.2 %fetch.1 = (bf16[4096,512]{1,0:T(8,128)(2,1)S(1)}, bf16[16,4224]{1,0:T(8,128)(2,1)S(1)}) custom-call(bf16[4096,512]{1,0:T(8,128)(2,1)} %head.1, bf16[16,4224]{1,0:T(8,128)(2,1)S(1)} %join.1.rows), custom_call_target="tpu_custom_call" | custom-call | bytes 8388608 | tf_op jit(solution)/shard_map/fetch/pallas_call | solution.py:142
  18.5 0.1 collective-permute-start.9
  18.5 1.6 %collective-permute-done.3.refs_0_ = bf16[16,4224]{1,0:T(8,128)(2,1)S(1)} collective-permute-done((bf16[16,4224]{1,0:T(8,128)(2,1)S(1)}, bf16[16,4224]{1,0:T(8,128)(2,1)S(1)}, u32[]{:S(2)}, u32[]{:S(2)}) %collective-permute-start.3) | collective-permute-done | bytes 135200 | tf_op jit(solution)/shard_map/ppermute | solution.py:247
  20.1 0.0 collective-permute-start.4
  20.1 0.8 %collective-permute-done.5.refs_1_ = bf16[16,4224]{1,0:T(8,128)(2,1)S(1)} collective-permute-done((bf16[16,4224]{1,0:T(8,128)(2,1)S(1)}, bf16[16,4224]{1,0:T(8,128)(2,1)S(1)}, u32[]{:S(2)}, u32[]{:S(2)}) %collective-permute-start.5) | collective-permute-done | bytes 135200 | tf_op jit(solution)/shard_map/ppermute | solution.py:247
  20.9 0.0 collective-permute-start.6
  20.9 0.0 collective-permute-done.7.refs_2_
  20.9 0.5 %collective-permute-start.8 = (bf16[16,4224]{1,0:T(8,128)(2,1)S(1)}, bf16[16,4224]{1,0:T(8,128)(2,1)S(1)}, u32[]{:S(2)}, u32[]{:S(2)}) collective-permute-start(bf16[16,4224]{1,0:T(8,128)(2,1)S(1)} %collective-permute-done.7.refs_2_), channel_id=1, source_target_pairs={{0,4},{4,0},{8,12},{12,8},{16,20},{20,16},{24,28},{28,24},{1,5},{5... | collective-permute-start | bytes 405512 | tf_op jit(solution)/shard_map/ppermute | solution.py:247
  21.4 1.0 %score.2.refs_4_ = f32[4,2,128]{2,1,0:T(2,128)S(1)} custom-call(bf16[4096,512]{1,0:T(8,128)(2,1)S(1)} %get-tuple-element.11.head, bf16[16,4224]{1,0:T(8,128)(2,1)S(1)} %collective-permute-done.3.refs_0_, bf16[16,4224]{1,0:T(8,128)(2,1)S(1)} %collective-permute-done.5.refs_1_, bf16[16,4224]{1,0:T(8,128)(2,1)S(1)} %collective-permute-done.7.refs_2_, ...), custom_call_target="tpu_custom_call" | custom-call | tf_op jit(solution)/shard_map/score/pallas_call | solution.py:194
  22.4 0.0 collective-permute-done.9.refs_3_
  22.5 0.0 collective-permute-done.4.refs_0_
  22.5 0.0 collective-permute-done.6.refs_1_
  22.5 0.0 collective-permute-done.8.refs_2_
  22.5 1.0 %score.3 = f32[8,4,2,128]{3,2,1,0:T(2,128)S(1)} custom-call(bf16[4096,512]{1,0:T(8,128)(2,1)S(1)} %get-tuple-element.11.head, bf16[16,4224]{1,0:T(8,128)(2,1)S(1)} %collective-permute-done.4.refs_0_, bf16[16,4224]{1,0:T(8,128)(2,1)S(1)} %collective-permute-done.6.refs_1_, bf16[16,4224]{1,0:T(8,128)(2,1)S(1)} %collective-permute-done.8.refs_2_, ...), custom_call_target="tpu_custom_call" | custom-call | tf_op jit(solution)/shard_map/score/pallas_call | solution.py:194
  23.5 10.2 %all_to_all.5.stats = f32[32,2,128]{2,1,0:T(2,128)S(1)} all-to-all(f32[32,2,128]{2,1,0:T(2,128)S(1)} %bitcast.2), channel_id=1, replica_groups=mesh['dp'=8,'tensor'=4] {'dp','tensor'}, dimensions={0} | all-to-all | bytes 65536 | tf_op jit(solution)/shard_map/all_to_all | solution.py:262
  33.8 0.7 %finish.1 = (f32[1,32]{1,0:T(1,128)}, f32[1,32]{1,0:T(1,128)}) custom-call(f32[32,2,128]{2,1,0:T(2,128)S(1)} %all_to_all.5.stats, f32[16,32]{1,0:T(8,128)S(1)} %get-tuple-element.13.place), custom_call_target="tpu_custom_call" | custom-call | tf_op jit(solution)/shard_map/finish/pallas_call | solution.py:231
Async XLA Ops:
  2.6 7.0 %collective-permute-start = (bf16[16,1024]{1,0:T(8,128)(2,1)S(1)}, bf16[16,1024]{1,0:T(8,128)(2,1)S(1)}, u32[]{:S(2)}, u32[]{:S(2)}) collective-permute-start(bf16[16,1024]{1,0:T(8,128)(2,1)S(1)} %get-tuple-element.8.refs_3_), channel_id=1, source_target_pairs={{0,3},{1,2},{2,1},{3,0},{4,7},{5,6},{6,5},{7,4},{8,11},{9,10},{10,... | collective-permute-start | bytes 98312 | tf_op jit(solution)/shard_map/ppermute | solution.py:247
  7.7 4.8 %collective-permute-start.1 = (bf16[16,1024]{1,0:T(8,128)(2,1)S(1)}, bf16[16,1024]{1,0:T(8,128)(2,1)S(1)}, u32[]{:S(2)}, u32[]{:S(2)}) collective-permute-start(bf16[16,1024]{1,0:T(8,128)(2,1)S(1)} %get-tuple-element.8.refs_3_), channel_id=1, source_target_pairs={{0,2},{1,3},{2,0},{3,1},{4,6},{5,7},{6,4},{7,5},{8,10},{9,11},{10,... | collective-permute-start | bytes 98312 | tf_op jit(solution)/shard_map/ppermute | solution.py:247
  7.7 4.8 %collective-permute-start.2 = (bf16[16,1024]{1,0:T(8,128)(2,1)S(1)}, bf16[16,1024]{1,0:T(8,128)(2,1)S(1)}, u32[]{:S(2)}, u32[]{:S(2)}) collective-permute-start(bf16[16,1024]{1,0:T(8,128)(2,1)S(1)} %get-tuple-element.8.refs_3_), channel_id=1, source_target_pairs={{0,1},{1,0},{2,3},{3,2},{4,5},{5,4},{6,7},{7,6},{8,9},{9,8},{10,11... | collective-permute-start | bytes 98312 | tf_op jit(solution)/shard_map/ppermute | solution.py:247
  12.7 7.4 %collective-permute-start.3 = (bf16[16,4224]{1,0:T(8,128)(2,1)S(1)}, bf16[16,4224]{1,0:T(8,128)(2,1)S(1)}, u32[]{:S(2)}, u32[]{:S(2)}) collective-permute-start(bf16[16,4224]{1,0:T(8,128)(2,1)S(1)} %join.1.rows), channel_id=1, source_target_pairs={{0,24},{4,28},{8,16},{12,20},{16,8},{20,12},{24,0},{28,4},{1,25},{... | collective-permute-start | bytes 405512 | tf_op jit(solution)/shard_map/ppermute | solution.py:247
  15.2 5.7 %collective-permute-start.5 = (bf16[16,4224]{1,0:T(8,128)(2,1)S(1)}, bf16[16,4224]{1,0:T(8,128)(2,1)S(1)}, u32[]{:S(2)}, u32[]{:S(2)}) collective-permute-start(bf16[16,4224]{1,0:T(8,128)(2,1)S(1)} %join.1.rows), channel_id=1, source_target_pairs={{0,16},{4,20},{8,24},{12,28},{16,0},{20,4},{24,8},{28,12},{1,17},{... | collective-permute-start | bytes 405512 | tf_op jit(solution)/shard_map/ppermute | solution.py:247
  15.7 5.2 %collective-permute-start.7 = (bf16[16,4224]{1,0:T(8,128)(2,1)S(1)}, bf16[16,4224]{1,0:T(8,128)(2,1)S(1)}, u32[]{:S(2)}, u32[]{:S(2)}) collective-permute-start(bf16[16,4224]{1,0:T(8,128)(2,1)S(1)} %join.1.rows), channel_id=1, source_target_pairs={{0,8},{4,12},{8,0},{12,4},{16,24},{20,28},{24,16},{28,20},{1,9},{5... | collective-permute-start | bytes 405512 | tf_op jit(solution)/shard_map/ppermute | solution.py:247
  18.5 4.0 %collective-permute-start.9 = (bf16[16,4224]{1,0:T(8,128)(2,1)S(1)}, bf16[16,4224]{1,0:T(8,128)(2,1)S(1)}, u32[]{:S(2)}, u32[]{:S(2)}) collective-permute-start(bf16[16,4224]{1,0:T(8,128)(2,1)S(1)} %get-tuple-element.12.refs_3_), channel_id=1, source_target_pairs={{0,4},{4,0},{8,12},{12,8},{16,20},{20,16},{24,28},{28,24},{1,5},{5... | collective-permute-start | bytes 405512 | tf_op jit(solution)/shard_map/ppermute | solution.py:247
  20.1 2.3 %collective-permute-start.4 = (bf16[16,4224]{1,0:T(8,128)(2,1)S(1)}, bf16[16,4224]{1,0:T(8,128)(2,1)S(1)}, u32[]{:S(2)}, u32[]{:S(2)}) collective-permute-start(bf16[16,4224]{1,0:T(8,128)(2,1)S(1)} %collective-permute-done.3.refs_0_), channel_id=1, source_target_pairs={{0,4},{4,0},{8,12},{12,8},{16,20},{20,16},{24,28},{28,24},{1,5},{5... | collective-permute-start | bytes 405512 | tf_op jit(solution)/shard_map/ppermute | solution.py:247
  20.9 1.6 %collective-permute-start.6 = (bf16[16,4224]{1,0:T(8,128)(2,1)S(1)}, bf16[16,4224]{1,0:T(8,128)(2,1)S(1)}, u32[]{:S(2)}, u32[]{:S(2)}) collective-permute-start(bf16[16,4224]{1,0:T(8,128)(2,1)S(1)} %collective-permute-done.5.refs_1_), channel_id=1, source_target_pairs={{0,4},{4,0},{8,12},{12,8},{16,20},{20,16},{24,28},{28,24},{1,5},{5... | collective-permute-start | bytes 405512 | tf_op jit(solution)/shard_map/ppermute | solution.py:247
  20.9 1.6 %collective-permute-start.8 = (bf16[16,4224]{1,0:T(8,128)(2,1)S(1)}, bf16[16,4224]{1,0:T(8,128)(2,1)S(1)}, u32[]{:S(2)}, u32[]{:S(2)}) collective-permute-start(bf16[16,4224]{1,0:T(8,128)(2,1)S(1)} %collective-permute-done.7.refs_2_), channel_id=1, source_target_pairs={{0,4},{4,0},{8,12},{12,8},{16,20},{20,16},{24,28},{28,24},{1,5},{5... | collective-permute-start | bytes 405512 | tf_op jit(solution)/shard_map/ppermute | solution.py:247

commit v4 on v2

--- a/solution.py
+++ b/solution.py
@@ -1,5 +1,3 @@
-import functools
-
 import jax
 import jax.numpy as jnp
 from jax import lax
@@ -13,7 +11,6 @@
 CODE = 128
 DIGIT = 64
 GROUP = 16
-CHUNK = 1024
 
 
 def vmem_limit(mebibytes):
@@ -152,8 +149,8 @@
     )(in_hbm(head), rows)
 
 
-def score_kernel(order, *refs):
-    dp = len(order)
+def score_kernel(*refs):
+    dp = len(refs) - 2
     pieces, (head, stats) = refs[:dp], refs[dp:]
     depth, vocab_width = head.shape
     live = pieces[0].shape[0]
@@ -161,10 +158,8 @@
     mine = lax.axis_index("dp")
     start = (mine * stats.shape[1] + lax.axis_index("tensor")) * vocab_width
 
-    logits = jnp.zeros((row_count, vocab_width), jnp.float32)
-    for k in range(0, depth, CHUNK):
-        normed = jnp.concatenate([piece[:, k : k + CHUNK] for piece in pieces], axis=0)
-        logits += jnp.dot(normed, head[k : k + CHUNK], preferred_element_type=jnp.float32)
+    normed = jnp.concatenate([piece[:, :depth] for piece in pieces], axis=0)
+    logits = jnp.dot(normed, head[...], preferred_element_type=jnp.float32)
     digits = jnp.concatenate([piece[:, depth:] for piece in pieces], axis=0).astype(jnp.float32)
     lane = lax.broadcasted_iota(jnp.int32, (row_count, CODE), 1)
     weight = jnp.where(lane == 0, 1.0, jnp.where(lane == 1, float(DIGIT), jnp.where(lane == 2, float(DIGIT * DIGIT), 0.0)))
@@ -180,18 +175,18 @@
     sums = jnp.zeros((row_count, CODE), jnp.float32)
     for group, value in enumerate((total, weighted, chosen)):
         sums = jnp.where(spot == GROUP * group, value, sums)
-    for i, d in enumerate(order):
+    for d in range(dp):
         for line, table in enumerate((tops, sums)):
-            packed = jnp.sum(table[i * live : (i + 1) * live], axis=0, keepdims=True)
+            packed = jnp.sum(table[d * live : (d + 1) * live], axis=0, keepdims=True)
             for t in range(stats.shape[1]):
                 stats[mine ^ d, t, line : line + 1] = packed
 
 
-def score(pieces, order, head, copies):
-    dp = len(order)
-    vmem = pl.BlockSpec(memory_space=pltpu.VMEM)
-    return pl.pallas_call(
-        functools.partial(score_kernel, order),
+def score(pieces, head, copies):
+    dp = len(pieces)
+    vmem = pl.BlockSpec(memory_space=pltpu.VMEM)
+    return pl.pallas_call(
+        score_kernel,
         out_shape=jax.ShapeDtypeStruct((dp, copies, 2, CODE), jnp.float32),
         in_specs=[vmem] * (dp + 1),
         out_specs=vmem,
@@ -256,8 +251,7 @@
     held, pieces[0] = fetch(head, rows)
     for d in range(0, dp, 2):
         pieces[d + 1] = swap(pieces[d], "dp", 1)
-    order = [0, 1] + [d + core for d in reversed(range(2, dp, 2)) for core in (0, 1)]
-    stats = score([pieces[d] for d in order], order, held, tensor)
+    stats = score([pieces[d] for d in range(dp)], held, tensor)
     stats = lax.all_to_all(stats.reshape(dp * tensor, 2, CODE), ("dp", "tensor"), 0, 0, tiled=True)
     return finish(stats, slots, offsets.shape[1])
 

time: 35.1 us -> 34.6 us (0.986)
  waiting for transfers between devices: 8.68 us -> 7.55 us
  starting transfers between devices: 9.39 us -> 9.89 us
    ppermute x10, waiting for transfers between devices: 8.68 us -> 7.55 us  [swap(): lax.ppermute(x, axis, [(i, i ^ distance) for i in range(lax.axis_size(axi...]
    ppermute x10, starting transfers between devices: 9.39 us -> 9.89 us  [swap(): lax.ppermute(x, axis, [(i, i ^ distance) for i in range(lax.axis_size(axi...]
  transfers between devices with their start and end apart: 10 -> 10, of which waited for: 6 -> 7; matrix products, arithmetic and copies ran while one was open for 0% -> 0% of each run, Pallas kernels for 6% -> 6%
where the time goes in v4:
time: 34.6 us; the launch traced here: 34.3 us
  blocking collectives  10.3 us (30%)
  starting transfers between devices  9.89 us (29%)
  waiting for transfers between devices  7.55 us (22%)
  Pallas kernels  5.32 us (15%)
  between operations  1.32 us (4%)
    all_to_all x1, blocking collectives, per_device(): lax.all_to_all(stats.reshape(dp * tensor, 2, CODE), ('dp', 'tensor'), 0,...  10.3 us
    ppermute x10, starting transfers between devices, swap(): lax.ppermute(x, axis, [(i, i ^ distance) for i in range(lax.axis_size(axi...  9.89 us
    ppermute x10, waiting for transfers between devices, swap(): lax.ppermute(x, axis, [(i, i ^ distance) for i in range(lax.axis_size(axi...  7.55 us
    pallas_call x1, Pallas kernels, fetch(): pl.pallas_call(fetch_kernel, out_shape=(pltpu.VMEM(head.shape, head.dtype...  2.21 us
    pallas_call x1, Pallas kernels, pick(): pl.pallas_call(pick_kernel, out_shape=(jax.ShapeDtypeStruct((LIVE, featur...  1.34 us
    pallas_call x1, Pallas kernels, score(): pl.pallas_call(score_kernel, out_shape=jax.ShapeDtypeStruct((dp, copies,...  0.9 us
    pallas_call x1, Pallas kernels, finish(): pl.pallas_call(finish_kernel, out_shape=(out, out), in_specs=[vmem, vmem]...  0.75 us
  transfers between devices with their start and end apart: 10, of which 7 were waited for; matrix products, arithmetic and copies ran while one was open for 0% of the time, Pallas kernels for 6%

profile of v4, /device:TPU:0, one launch (start us, length us, event | category | flops | bytes accessed | tf_op | source)
XLA Modules:
  0.0 34.3 jit_solution(3263348915759746691)
XLA Ops:
  1.3 1.3 %pick.1 = (bf16[16,1024]{1,0:T(8,128)(2,1)S(1)}, bf16[16,128]{1,0:T(8,128)(2,1)S(1)}, f32[16,32]{1,0:T(8,128)S(1)}, f32[1,4096]{1,0:T(1,128)S(1)}) custom-call(s32[1]{0:T(128)S(6)} %copy.9.lengths, s32[1,32]{1,0:T(1,128)} %offsets.1, s32[1,32]{1,0:T(1,128)} %targets.1, s32[1,32]{1,0:T(1,128)} %mask.1, f32[1,4096]{1,0:T(1,128)} %bitcast.3, ...), custom_call_target="tpu_custom_call" | custom-call | tf_op jit(solution)/shard_map/pick/pallas_call | solution.py:72
  2.6 5.1 %collective-permute-start.2 = (bf16[16,1024]{1,0:T(8,128)(2,1)S(1)}, bf16[16,1024]{1,0:T(8,128)(2,1)S(1)}, u32[]{:S(2)}, u32[]{:S(2)}) collective-permute-start(bf16[16,1024]{1,0:T(8,128)(2,1)S(1)} %get-tuple-element.8.refs_0_), channel_id=1, source_target_pairs={{0,3},{1,2},{2,1},{3,0},{4,7},{5,6},{6,5},{7,4},{8,11},{9,10},{10,... | collective-permute-start | bytes 98312 | tf_op jit(solution)/shard_map/ppermute | solution.py:241
  7.7 0.0 collective-permute-start.1
  7.7 0.6 %collective-permute-start = (bf16[16,1024]{1,0:T(8,128)(2,1)S(1)}, bf16[16,1024]{1,0:T(8,128)(2,1)S(1)}, u32[]{:S(2)}, u32[]{:S(2)}) collective-permute-start(bf16[16,1024]{1,0:T(8,128)(2,1)S(1)} %get-tuple-element.8.refs_0_), channel_id=1, source_target_pairs={{0,1},{1,0},{2,3},{3,2},{4,5},{5,4},{6,7},{7,6},{8,9},{9,8},{10,11... | collective-permute-start | bytes 98312 | tf_op jit(solution)/shard_map/ppermute | solution.py:241
  8.4 1.3 %collective-permute-done.2.refs_3_ = bf16[16,1024]{1,0:T(8,128)(2,1)S(1)} collective-permute-done((bf16[16,1024]{1,0:T(8,128)(2,1)S(1)}, bf16[16,1024]{1,0:T(8,128)(2,1)S(1)}, u32[]{:S(2)}, u32[]{:S(2)}) %collective-permute-start.2) | collective-permute-done | bytes 32800 | tf_op jit(solution)/shard_map/ppermute | solution.py:241
  9.6 2.9 %collective-permute-done.1.refs_2_ = bf16[16,1024]{1,0:T(8,128)(2,1)S(1)} collective-permute-done((bf16[16,1024]{1,0:T(8,128)(2,1)S(1)}, bf16[16,1024]{1,0:T(8,128)(2,1)S(1)}, u32[]{:S(2)}, u32[]{:S(2)}) %collective-permute-start.1) | collective-permute-done | bytes 32800 | tf_op jit(solution)/shard_map/ppermute | solution.py:241
  12.6 0.0 collective-permute-done.refs_1_
  12.6 0.1 join.1.rows
  12.7 2.5 %collective-permute-start.8 = (bf16[16,4224]{1,0:T(8,128)(2,1)S(1)}, bf16[16,4224]{1,0:T(8,128)(2,1)S(1)}, u32[]{:S(2)}, u32[]{:S(2)}) collective-permute-start(bf16[16,4224]{1,0:T(8,128)(2,1)S(1)} %join.1.rows), channel_id=1, source_target_pairs={{0,24},{4,28},{8,16},{12,20},{16,8},{20,12},{24,0},{28,4},{1,25},{... | collective-permute-start | bytes 405512 | tf_op jit(solution)/shard_map/ppermute | solution.py:241
  15.2 0.5 %collective-permute-start.6 = (bf16[16,4224]{1,0:T(8,128)(2,1)S(1)}, bf16[16,4224]{1,0:T(8,128)(2,1)S(1)}, u32[]{:S(2)}, u32[]{:S(2)}) collective-permute-start(bf16[16,4224]{1,0:T(8,128)(2,1)S(1)} %join.1.rows), channel_id=1, source_target_pairs={{0,16},{4,20},{8,24},{12,28},{16,0},{20,4},{24,8},{28,12},{1,17},{... | collective-permute-start | bytes 405512 | tf_op jit(solution)/shard_map/ppermute | solution.py:241
  15.7 0.5 %collective-permute-start.4 = (bf16[16,4224]{1,0:T(8,128)(2,1)S(1)}, bf16[16,4224]{1,0:T(8,128)(2,1)S(1)}, u32[]{:S(2)}, u32[]{:S(2)}) collective-permute-start(bf16[16,4224]{1,0:T(8,128)(2,1)S(1)} %join.1.rows), channel_id=1, source_target_pairs={{0,8},{4,12},{8,0},{12,4},{16,24},{20,28},{24,16},{28,20},{1,9},{5... | collective-permute-start | bytes 405512 | tf_op jit(solution)/shard_map/ppermute | solution.py:241
  16.3 2.2 %fetch.1 = (bf16[4096,512]{1,0:T(8,128)(2,1)S(1)}, bf16[16,4224]{1,0:T(8,128)(2,1)S(1)}) custom-call(bf16[4096,512]{1,0:T(8,128)(2,1)} %head.1, bf16[16,4224]{1,0:T(8,128)(2,1)S(1)} %join.1.rows), custom_call_target="tpu_custom_call" | custom-call | bytes 8388608 | tf_op jit(solution)/shard_map/fetch/pallas_call | solution.py:140
  18.5 0.1 collective-permute-start.3
  18.5 1.6 %collective-permute-done.8.refs_6_ = bf16[16,4224]{1,0:T(8,128)(2,1)S(1)} collective-permute-done((bf16[16,4224]{1,0:T(8,128)(2,1)S(1)}, bf16[16,4224]{1,0:T(8,128)(2,1)S(1)}, u32[]{:S(2)}, u32[]{:S(2)}) %collective-permute-start.8) | collective-permute-done | bytes 135200 | tf_op jit(solution)/shard_map/ppermute | solution.py:241
  20.1 0.0 collective-permute-start.9
  20.1 0.8 %collective-permute-done.6.refs_4_ = bf16[16,4224]{1,0:T(8,128)(2,1)S(1)} collective-permute-done((bf16[16,4224]{1,0:T(8,128)(2,1)S(1)}, bf16[16,4224]{1,0:T(8,128)(2,1)S(1)}, u32[]{:S(2)}, u32[]{:S(2)}) %collective-permute-start.6) | collective-permute-done | bytes 135200 | tf_op jit(solution)/shard_map/ppermute | solution.py:241
  20.9 0.0 collective-permute-start.7
  20.9 0.0 collective-permute-done.4.refs_2_
  20.9 0.5 %collective-permute-start.5 = (bf16[16,4224]{1,0:T(8,128)(2,1)S(1)}, bf16[16,4224]{1,0:T(8,128)(2,1)S(1)}, u32[]{:S(2)}, u32[]{:S(2)}) collective-permute-start(bf16[16,4224]{1,0:T(8,128)(2,1)S(1)} %collective-permute-done.4.refs_2_), channel_id=1, source_target_pairs={{0,4},{4,0},{8,12},{12,8},{16,20},{20,16},{24,28},{28,24},{1,5},{5... | collective-permute-start | bytes 405512 | tf_op jit(solution)/shard_map/ppermute | solution.py:241
  21.4 0.0 collective-permute-done.3.refs_1_
  21.4 0.1 collective-permute-done.9.refs_7_
  21.5 0.8 %collective-permute-done.7.refs_5_ = bf16[16,4224]{1,0:T(8,128)(2,1)S(1)} collective-permute-done((bf16[16,4224]{1,0:T(8,128)(2,1)S(1)}, bf16[16,4224]{1,0:T(8,128)(2,1)S(1)}, u32[]{:S(2)}, u32[]{:S(2)}) %collective-permute-start.7) | collective-permute-done | bytes 135200 | tf_op jit(solution)/shard_map/ppermute | solution.py:241
  22.2 0.2 collective-permute-done.5.refs_3_
  22.4 0.9 %score.1 = f32[8,4,2,128]{3,2,1,0:T(2,128)S(1)} custom-call(bf16[16,4224]{1,0:T(8,128)(2,1)S(1)} %get-tuple-element.11.refs_0_, bf16[16,4224]{1,0:T(8,128)(2,1)S(1)} %collective-permute-done.3.refs_1_, bf16[16,4224]{1,0:T(8,128)(2,1)S(1)} %collective-permute-done.4.refs_2_, bf16[16,4224]{1,0:T(8,128)(2,1)S(1)} %collective-permute-done.5.refs_3_, ...), custom_call_target="tpu_custom_call" | custom-call | tf_op jit(solution)/shard_map/score/pallas_call | solution.py:188
  23.3 10.3 %all_to_all.5.stats = f32[32,2,128]{2,1,0:T(2,128)S(1)} all-to-all(f32[32,2,128]{2,1,0:T(2,128)S(1)} %bitcast.2), channel_id=1, replica_groups=mesh['dp'=8,'tensor'=4] {'dp','tensor'}, dimensions={0} | all-to-all | bytes 65536 | tf_op jit(solution)/shard_map/all_to_all | solution.py:255
  33.6 0.7 %finish.1 = (f32[1,32]{1,0:T(1,128)}, f32[1,32]{1,0:T(1,128)}) custom-call(f32[32,2,128]{2,1,0:T(2,128)S(1)} %all_to_all.5.stats, f32[16,32]{1,0:T(8,128)S(1)} %get-tuple-element.13.place), custom_call_target="tpu_custom_call" | custom-call | tf_op jit(solution)/shard_map/finish/pallas_call | solution.py:225
Async XLA Ops:
  2.6 7.0 %collective-permute-start.2 = (bf16[16,1024]{1,0:T(8,128)(2,1)S(1)}, bf16[16,1024]{1,0:T(8,128)(2,1)S(1)}, u32[]{:S(2)}, u32[]{:S(2)}) collective-permute-start(bf16[16,1024]{1,0:T(8,128)(2,1)S(1)} %get-tuple-element.8.refs_0_), channel_id=1, source_target_pairs={{0,3},{1,2},{2,1},{3,0},{4,7},{5,6},{6,5},{7,4},{8,11},{9,10},{10,... | collective-permute-start | bytes 98312 | tf_op jit(solution)/shard_map/ppermute | solution.py:241
  7.7 4.8 %collective-permute-start.1 = (bf16[16,1024]{1,0:T(8,128)(2,1)S(1)}, bf16[16,1024]{1,0:T(8,128)(2,1)S(1)}, u32[]{:S(2)}, u32[]{:S(2)}) collective-permute-start(bf16[16,1024]{1,0:T(8,128)(2,1)S(1)} %get-tuple-element.8.refs_0_), channel_id=1, source_target_pairs={{0,2},{1,3},{2,0},{3,1},{4,6},{5,7},{6,4},{7,5},{8,10},{9,11},{10,... | collective-permute-start | bytes 98312 | tf_op jit(solution)/shard_map/ppermute | solution.py:241
  7.7 4.8 %collective-permute-start = (bf16[16,1024]{1,0:T(8,128)(2,1)S(1)}, bf16[16,1024]{1,0:T(8,128)(2,1)S(1)}, u32[]{:S(2)}, u32[]{:S(2)}) collective-permute-start(bf16[16,1024]{1,0:T(8,128)(2,1)S(1)} %get-tuple-element.8.refs_0_), channel_id=1, source_target_pairs={{0,1},{1,0},{2,3},{3,2},{4,5},{5,4},{6,7},{7,6},{8,9},{9,8},{10,11... | collective-permute-start | bytes 98312 | tf_op jit(solution)/shard_map/ppermute | solution.py:241
  12.7 7.4 %collective-permute-start.8 = (bf16[16,4224]{1,0:T(8,128)(2,1)S(1)}, bf16[16,4224]{1,0:T(8,128)(2,1)S(1)}, u32[]{:S(2)}, u32[]{:S(2)}) collective-permute-start(bf16[16,4224]{1,0:T(8,128)(2,1)S(1)} %join.1.rows), channel_id=1, source_target_pairs={{0,24},{4,28},{8,16},{12,20},{16,8},{20,12},{24,0},{28,4},{1,25},{... | collective-permute-start | bytes 405512 | tf_op jit(solution)/shard_map/ppermute | solution.py:241
  15.2 5.7 %collective-permute-start.6 = (bf16[16,4224]{1,0:T(8,128)(2,1)S(1)}, bf16[16,4224]{1,0:T(8,128)(2,1)S(1)}, u32[]{:S(2)}, u32[]{:S(2)}) collective-permute-start(bf16[16,4224]{1,0:T(8,128)(2,1)S(1)} %join.1.rows), channel_id=1, source_target_pairs={{0,16},{4,20},{8,24},{12,28},{16,0},{20,4},{24,8},{28,12},{1,17},{... | collective-permute-start | bytes 405512 | tf_op jit(solution)/shard_map/ppermute | solution.py:241
  15.7 5.2 %collective-permute-start.4 = (bf16[16,4224]{1,0:T(8,128)(2,1)S(1)}, bf16[16,4224]{1,0:T(8,128)(2,1)S(1)}, u32[]{:S(2)}, u32[]{:S(2)}) collective-permute-start(bf16[16,4224]{1,0:T(8,128)(2,1)S(1)} %join.1.rows), channel_id=1, source_target_pairs={{0,8},{4,12},{8,0},{12,4},{16,24},{20,28},{24,16},{28,20},{1,9},{5... | collective-permute-start | bytes 405512 | tf_op jit(solution)/shard_map/ppermute | solution.py:241
  18.5 2.9 %collective-permute-start.3 = (bf16[16,4224]{1,0:T(8,128)(2,1)S(1)}, bf16[16,4224]{1,0:T(8,128)(2,1)S(1)}, u32[]{:S(2)}, u32[]{:S(2)}) collective-permute-start(bf16[16,4224]{1,0:T(8,128)(2,1)S(1)} %get-tuple-element.11.refs_0_), channel_id=1, source_target_pairs={{0,4},{4,0},{8,12},{12,8},{16,20},{20,16},{24,28},{28,24},{1,5},{5... | collective-permute-start | bytes 405512 | tf_op jit(solution)/shard_map/ppermute | solution.py:241
  20.1 1.4 %collective-permute-start.9 = (bf16[16,4224]{1,0:T(8,128)(2,1)S(1)}, bf16[16,4224]{1,0:T(8,128)(2,1)S(1)}, u32[]{:S(2)}, u32[]{:S(2)}) collective-permute-start(bf16[16,4224]{1,0:T(8,128)(2,1)S(1)} %collective-permute-done.8.refs_6_), channel_id=1, source_target_pairs={{0,4},{4,0},{8,12},{12,8},{16,20},{20,16},{24,28},{28,24},{1,5},{5... | collective-permute-start | bytes 405512 | tf_op jit(solution)/shard_map/ppermute | solution.py:241
  20.9 1.4 %collective-permute-start.7 = (bf16[16,4224]{1,0:T(8,128)(2,1)S(1)}, bf16[16,4224]{1,0:T(8,128)(2,1)S(1)}, u32[]{:S(2)}, u32[]{:S(2)}) collective-permute-start(bf16[16,4224]{1,0:T(8,128)(2,1)S(1)} %collective-permute-done.6.refs_4_), channel_id=1, source_target_pairs={{0,4},{4,0},{8,12},{12,8},{16,20},{20,16},{24,28},{28,24},{1,5},{5... | collective-permute-start | bytes 405512 | tf_op jit(solution)/shard_map/ppermute | solution.py:241
  20.9 1.5 %collective-permute-start.5 = (bf16[16,4224]{1,0:T(8,128)(2,1)S(1)}, bf16[16,4224]{1,0:T(8,128)(2,1)S(1)}, u32[]{:S(2)}, u32[]{:S(2)}) collective-permute-start(bf16[16,4224]{1,0:T(8,128)(2,1)S(1)} %collective-permute-done.4.refs_2_), channel_id=1, source_target_pairs={{0,4},{4,0},{8,12},{12,8},{16,20},{20,16},{24,28},{28,24},{1,5},{5... | collective-permute-start | bytes 405512 | tf_op jit(solution)/shard_map/ppermute | solution.py:241
